TPU v7x, 256 devices: a whole 4x4x8 slice. The times are simulated.
256 devices in a mesh: seq: 32 (over z, x), head: 8 (over y, core).
Axes of the slice: x: 4, y: 4, z: 8, core: 2. Of those that a mesh axis runs over, the one named last changes fastest.
Arguments:
- tokens: bfloat16 [8192, 2048], P('seq', 'head'), may hold values from -6 to 6
- in_weight: bfloat16 [2048, 12288], P(None, 'head'), may hold values from -0.125 to 0.125
- gate_weight: bfloat16 [2048, 64], P(None, 'head'), may hold values from -0.125 to 0.125
- conv_weight: bfloat16 [4, 16, 512], P(None, 'head'), may hold values from -3 to 3
- decay_scale: float32 [32], P('head'), may hold values from 1e-05 to 0.1
- dt_bias: float32 [32], P('head'), may hold values from -3 to 1
- beta_shift: float32 [32], P('head'), may hold values from -1 to 6
- norm_gain: float32 [128], replicated, may hold values from 0.1 to 1.9
- out_weight: bfloat16 [4096, 2048], P('head'), may hold values from -0.09375 to 0.09375
Outputs:
- layer_out: bfloat16 [8192, 2048], P('seq', 'head')
All inputs are finite; a program needn't handle non-finite values.
Results may differ from a plain program's by a relative error of at most 0.02.
Values may be sent and summed in bfloat16 or wider, within the bound.
A program may use at most 128 MiB of HBM per device.

v0:
```python
import jax
import jax.numpy as jnp
from jax import lax
from jax.sharding import PartitionSpec as P

DK = 128
DV = 128
SPAN = 128


PRECISE = lax.Precision.HIGHEST
epsilon = 1e-06


def passed_along(block, axis, distance):
    devices = range(lax.axis_size(axis))
    route = [(i - distance, i) for i in devices if i - distance in devices]
    return lax.ppermute(block, axis, route)


def to_blocks(source):
    block_count = source.shape[0] // SPAN
    shaped = source.reshape((block_count, SPAN) + source.shape[1:])
    if source.ndim == 2:
        return shaped.transpose(0, 2, 1)
    return shaped.transpose(0, 2, 1, 3)


def span_pass(query_blocks, key_blocks, value_blocks, gate_blocks, beta_blocks, initial):
    block_len = gate_blocks.shape[-1]
    row_index = lax.broadcasted_iota(jnp.int32, (block_len, block_len), 0)
    col_index = lax.broadcasted_iota(jnp.int32, (block_len, block_len), 1)
    on_lower = col_index <= row_index
    below_diag = col_index < row_index
    lower_ones = on_lower.astype(jnp.float32)
    unit_matrix = jnp.eye(block_len, dtype=jnp.float32)

    def advance(carried, block_data):
        block_query, block_keys, block_values, block_gates, block_beta = block_data
        cumulative = jnp.einsum("hj,tj->ht", block_gates, lower_ones, precision=PRECISE)
        log_gap = cumulative[:, :, None] - cumulative[:, None, :]
        decay_ratio = jnp.where(on_lower, jnp.exp(jnp.where(on_lower, log_gap, 0.0)), 0.0)
        key_inner = jnp.einsum("htd,hjd->htj", block_keys, block_keys, precision=PRECISE)
        system = unit_matrix + jnp.where(
            below_diag, block_beta[:, :, None] * decay_ratio * key_inner, 0.0
        )
        start_decay = jnp.exp(cumulative)
        state_keys = jnp.einsum("htd,hwd->htw", block_keys, carried, precision=PRECISE)
        right_side = block_beta[:, :, None] * (block_values - start_decay[:, :, None] * state_keys)
        update = jax.scipy.linalg.solve_triangular(
            system, right_side, lower=True, unit_diagonal=True
        )
        end_decay = jnp.exp(cumulative[:, -1:] - cumulative)
        renewed = carried * start_decay[:, -1][:, None, None] + jnp.einsum(
            "htw,htd->hwd", update * end_decay[:, :, None], block_keys, precision=PRECISE
        )
        scores = (
            jnp.einsum("htd,hjd->htj", block_query, block_keys, precision=PRECISE) * decay_ratio
        )
        result = start_decay[:, :, None] * jnp.einsum(
            "htd,hwd->htw", block_query, carried, precision=PRECISE
        )
        result = result + jnp.einsum("htj,hjw->htw", scores, update, precision=PRECISE)
        return (renewed, result)

    return lax.scan(
        advance, initial, (query_blocks, key_blocks, value_blocks, gate_blocks, beta_blocks)
    )


def per_device(
    tokens,
    in_weight,
    gate_weight,
    conv_weight,
    decay_scale,
    dt_bias,
    beta_shift,
    norm_gain,
    out_weight,
):
    length = tokens.shape[0]
    group_width = 2 * DK + 4 * DV
    conv_width = 2 * DK + 2 * DV
    groups = in_weight.shape[1] // group_width
    head_count = 2 * groups
    pieces = lax.all_gather(tokens, "head", axis=1, tiled=True)
    projected = jnp.dot(pieces, in_weight, preferred_element_type=jnp.float32)
    gating = jnp.dot(pieces, gate_weight, preferred_element_type=jnp.float32)
    mixed = projected.astype(jnp.bfloat16).reshape(length, groups, group_width)
    conv_part = mixed[:, :, :conv_width]
    gate_part = mixed[:, :, conv_width:]
    taps = conv_weight.shape[0]
    prior_rows = passed_along(conv_part[length - (taps - 1) :], "seq", 1)
    extended = jnp.concatenate([prior_rows, conv_part], 0).astype(jnp.float32)
    filters = conv_weight.astype(jnp.float32)
    summed = filters[0] * extended[0:length]
    for offset in range(1, taps):
        summed = summed + filters[offset] * extended[offset : offset + length]
    filtered = jax.nn.silu(summed)
    query_rows = filtered[:, :, :DK]
    key_rows = filtered[:, :, DK : 2 * DK]
    value_rows = filtered[:, :, 2 * DK :].reshape(length, head_count, DV)
    query_rows = (
        query_rows
        / jnp.sqrt(jnp.sum(query_rows * query_rows, -1, keepdims=True) + epsilon)
        * DK ** (-0.5)
    )
    key_rows = key_rows / jnp.sqrt(jnp.sum(key_rows * key_rows, -1, keepdims=True) + epsilon)
    query_rows = jnp.repeat(query_rows, 2, axis=1)
    key_rows = jnp.repeat(key_rows, 2, axis=1)
    grouped = gating.reshape(length, groups, 4)
    beta_rate = jax.nn.sigmoid(grouped[:, :, :2].reshape(length, head_count) - beta_shift)
    log_gate = -decay_scale * jax.nn.softplus(
        grouped[:, :, 2:].reshape(length, head_count) + dt_bias
    )
    query_blocks = to_blocks(query_rows)
    key_blocks = to_blocks(key_rows)
    value_blocks = to_blocks(value_rows)
    gate_blocks = to_blocks(log_gate)
    beta_blocks = to_blocks(beta_rate)
    padding = jnp.zeros(value_blocks.shape[:3] + (DK,), jnp.float32)
    joined_values = jnp.concatenate([value_blocks, padding], -1)
    identity_block = jnp.broadcast_to(jnp.eye(DK, dtype=jnp.float32), (head_count, DK, DK))
    empty_state = jnp.zeros((head_count, DV, DK), jnp.float32)
    joined_start = jnp.concatenate([empty_state, identity_block], 1)
    joined_end, joined_out = span_pass(
        query_blocks, key_blocks, joined_values, gate_blocks, beta_blocks, joined_start
    )
    local_map = joined_end[:, DV:, :]
    local_shift = joined_end[:, :DV, :]
    gathered = (
        lax.all_gather(local_map[None].astype(jnp.bfloat16), "seq", axis=0, tiled=True).astype(
            jnp.float32
        ),
        lax.all_gather(local_shift[None].astype(jnp.bfloat16), "seq", axis=0, tiled=True).astype(
            jnp.float32
        ),
    )
    position = lax.axis_index("seq")

    def fold_step(offset, running):
        advanced = (
            jnp.einsum("hwd,hde->hwe", running, gathered[0][offset], precision=PRECISE)
            + gathered[1][offset]
        )
        return jnp.where(offset < position, advanced, running)

    start_state = lax.fori_loop(0, lax.axis_size("seq"), fold_step, empty_state)
    out_blocks = joined_out[..., :DV] + jnp.einsum(
        "nhtd,hwd->nhtw", joined_out[..., DV:], start_state, precision=PRECISE
    )
    attended = out_blocks.transpose(0, 2, 1, 3).reshape(length, head_count, DV)
    output_gate = gate_part.reshape(length, head_count, DV).astype(jnp.float32)
    scale_back = 1.0 / jnp.sqrt(jnp.mean(attended * attended, -1, keepdims=True) + epsilon)
    hidden = (attended * scale_back * norm_gain * jax.nn.silu(output_gate)).astype(jnp.bfloat16)
    hidden = hidden.reshape(length, head_count * DV)
    partial_value = jnp.dot(hidden, out_weight, preferred_element_type=jnp.float32)
    return lax.psum_scatter(
        partial_value.astype(jnp.bfloat16), "head", scatter_dimension=1, tiled=True
    )


def solution(mesh):
    in_specs = (
        P("seq", "head"),
        P(None, "head"),
        P(None, "head"),
        P(None, "head", None),
        P("head"),
        P("head"),
        P("head"),
        P(),
        P("head", None),
    )
    out_specs = P("seq", "head")
    return jax.shard_map(
        per_device, mesh=mesh, in_specs=in_specs, out_specs=out_specs, check_vma=False
    )
```

profile of v0, /device:TPU:224, one launch (start us, length us, event | category | flops | bytes accessed | tf_op | source)
XLA Modules:
  0.0 479.3 jit_solution(36207665171444987)
XLA Ops:
  8.8 26.8 %all-gather.6.cloned.1.call-done = bf16[256,2048]{1,0:T(8,128)(2,1)} async-done(((bf16[256,256]{1,0:T(8,128)(2,1)}), bf16[256,2048]{1,0:T(8,128)(2,1)}) %all-gather.6.cloned.1.call-update) | async-done | bytes 1048592 | tf_op jit(solution)/shard_map/all_gather | solution.py:87
  35.6 5.8 %convolution_convert_fusion.1 = bf16[256,1536]{1,0:T(8,128)(2,1)} fusion(bf16[256,2048]{1,0:T(8,128)(2,1)} %all-gather.6.cloned.1.call-done, bf16[2048,1536]{1,0:T(8,128)(2,1)} %param.14), kind=kOutput, calls=%fused_computation.69 | convolution fusion | flops 1611005952 | bytes 8126464 | tf_op jit(solution)/shard_map/dot_general | solution.py:88
  41.4 2.3 reshape.95
  44.7 3.5 collective-permute-start
  48.3 1.6 fusion.70
  51.2 2.0 copy.70
  53.2 4.3 collective-permute-done
  57.5 1.4 maximum_convert_fusion
  58.9 1.6 divide_multiply_fusion
  62.5 1.8 copy.41
  65.4 2.4 concatenate.11
  69.4 107.2 %while.28 = (s32[]{:T(128)}, f32[4,256,128]{2,1,0:T(8,128)S(1)}, f32[2,4,128,256]{3,2,1,0:T(8,128)}, f32[2,4,128]{2,0,1:T(2,128)S(1)}, f32[2,4,128]{2,0,1:T(2,12...) while((s32[]{:T(128)}, f32[4,256,128]{2,1,0:T(8,128)S(1)}, ...), condition=%wide.region_3.4_spmd.clone.clone, body=%wide.region_2.3_spmd.clone.clone.sunk | while | flops 1210794624 | bytes 24535340 | solution.py:66
  69.9 1.8 constant_dynamic-slice_fusion.7
  72.7 1.7 fusion.123
  74.6 2.5 fusion.125
  77.1 40.1 %custom-call.9 = f32[4,1,128,128]{2,3,1,0:T(8,128)S(1)} custom-call(f32[4,1,128,128]{3,2,1,0:T(8,128)} %fusion.125), custom_call_target="InvertDiagBlocksLowerTriangular" | custom-call | tf_op jit(solution)/shard_map/while/body/eval_jaxpr/jit(_solve_triangular)/vmap()/triangular_solve | solution.py:50
  117.9 1.6 convolution_multiply_fusion.6
  123.5 1.8 constant_dynamic-slice_fusion.7
  126.3 1.7 fusion.123
  128.2 2.5 fusion.125
  130.7 40.1 %custom-call.9 = f32[4,1,128,128]{2,3,1,0:T(8,128)S(1)} custom-call(f32[4,1,128,128]{3,2,1,0:T(8,128)} %fusion.125), custom_call_target="InvertDiagBlocksLowerTriangular" | custom-call | tf_op jit(solution)/shard_map/while/body/eval_jaxpr/jit(_solve_triangular)/vmap()/triangular_solve | solution.py:50
  171.5 1.6 convolution_multiply_fusion.6
  175.4 1.3 convolution_add_fusion.3
  179.6 2.6 copy.48
  182.2 76.2 %all-gather.10.cloned.1.call-done = bf16[128,128,128]{2,1,0:T(8,128)(2,1)} async-done(((bf16[4,128,128]{2,1,0:T(8,128)(2,1)}), bf16[128,128,128]{2,1,0:T(8,128)(2,1)}) %all-gather.10.cloned.1.call-update) | async-done | bytes 4194320 | tf_op jit(solution)/shard_map/all_gather | solution.py:136
  258.4 6.5 %convert.10 = f32[32,4,128,128]{3,2,1,0:T(8,128)} convert(bf16[32,4,128,128]{3,2,1,0:T(8,128)(2,1)} %bitcast.168) | non-fusion elementwise | flops 2097152 | bytes 12582912 | tf_op jit(solution)/shard_map/convert_element_type | solution.py:136
  264.9 75.3 %all-gather.8.cloned.1.call-done = bf16[128,128,128]{2,1,0:T(8,128)(2,1)} async-done(((bf16[4,128,128]{2,1,0:T(8,128)(2,1)}), bf16[128,128,128]{2,1,0:T(8,128)(2,1)}) %all-gather.8.cloned.1.call-update) | async-done | bytes 4194320 | tf_op jit(solution)/shard_map/all_gather | solution.py:133
  340.2 6.5 %convert.9 = f32[32,4,128,128]{3,2,1,0:T(8,128)} convert(bf16[32,4,128,128]{3,2,1,0:T(8,128)(2,1)} %bitcast.169) | non-fusion elementwise | flops 2097152 | bytes 12582912 | tf_op jit(solution)/shard_map/convert_element_type | solution.py:133
  346.7 87.1 %while.29 = (s32[]{:T(128)}, f32[4,128,128]{1,2,0:T(8,128)S(1)}, s32[]{:T(128)}, f32[32,4,128,128]{3,2,1,0:T(8,128)}, f32[32,4,128,128]{3,2,1,0:T(8,128)}, /*index=5*/s32[]{:T(128)}, s32[]{:T(128)}) while((s32[]{:T(128)}, f32[4,128,128]{1,2,0:T(8,128)S(1)}, s32[]{:T(128)}, f32[32,4,128,128]{3,2,1,0:T(8,128)}, ...), condition=%wide.region_5.6_spmd.clone, body=%wide.region_4.5_spmd.clone.sunk | while | flops 100925440 | bytes 2885731 | solution.py:149
  347.8 1.6 fusion.130
  350.5 1.6 fusion.130
  353.3 1.6 fusion.130
  356.0 1.6 fusion.130
  358.7 1.6 fusion.130
  361.4 1.6 fusion.130
  364.2 1.6 fusion.130
  366.9 1.6 fusion.130
  369.6 1.6 fusion.130
  372.3 1.6 fusion.130
  375.1 1.6 fusion.130
  377.8 1.6 fusion.130
  380.5 1.6 fusion.130
  383.2 1.6 fusion.130
  385.9 1.6 fusion.130
  388.7 1.6 fusion.130
  391.4 1.6 fusion.130
  394.1 1.6 fusion.130
  396.8 1.6 fusion.130
  399.6 1.6 fusion.130
  402.3 1.6 fusion.130
  405.0 1.6 fusion.130
  407.7 1.6 fusion.130
  410.5 1.6 fusion.130
  413.2 1.6 fusion.130
  415.9 1.6 fusion.130
  418.6 1.6 fusion.130
  421.4 1.6 fusion.130
  424.1 1.6 fusion.130
  426.8 1.6 fusion.130
  429.5 1.6 fusion.130
  432.2 1.6 fusion.130
  433.8 1.9 multiply_reduce_fusion
  437.2 2.8 convolution_convert_fusion
  440.0 32.7 %reduce-scatter.2.cloned.1.call-done = bf16[256,256]{1,0:T(8,128)(2,1)} async-done(((bf16[256,2048]{1,0:T(8,128)(2,1)}), bf16[256,256]{1,0:T(8,128)(2,1)}) %reduce-scatter.2.cloned.1.call-update) | async-done | bytes 131088 | tf_op jit(solution)/shard_map/reduce_scatter | solution.py:159
  (194 shorter events, 59.8 us)
Async XLA Ops:
  6.5 430.7 %copy-start = (bf16[512,2048]{1,0:T(8,128)(2,1)S(1)}, bf16[512,2048]{1,0:T(8,128)(2,1)}, u32[]{:S(2)}) copy-start(bf16[512,2048]{1,0:T(8,128)(2,1)} %param.21) | copy-start | bytes 6291460
  6.5 29.0 %all-gather.6.cloned.1.call-start = ((), (), s32[]{:S(2)}) async-start(), calls=%async_computation.1 | async-start | bytes 1179648 | tf_op jit(solution)/shard_map/all_gather | solution.py:87
  7.3 251.1 %all-gather.10.cloned.1.call-start = ((), (), s32[]{:S(2)}) async-start(), calls=%async_computation.4 | async-start | bytes 4325376 | tf_op jit(solution)/shard_map/all_gather | solution.py:136
  8.8 39.5 %copy-start.7 = (bf16[2048,8]{0,1:T(8,128)(2,1)S(1)}, bf16[2048,8]{0,1:T(8,128)(2,1)}, u32[]{:S(2)}) copy-start(bf16[2048,8]{0,1:T(8,128)(2,1)} %param.15) | copy-start | bytes 98308
  41.4 8.6 %copy-start.8 = (f32[4]{0:T(128)S(1)}, f32[4]{0:T(128)}, u32[]{:S(2)}) copy-start(f32[4]{0:T(128)} %param.18) | copy-start | bytes 52
  41.4 8.6 %copy-start.9 = (f32[4]{0:T(128)S(1)}, f32[4]{0:T(128)}, u32[]{:S(2)}) copy-start(f32[4]{0:T(128)} %param.19) | copy-start | bytes 52
  43.7 15.3 %copy-start.3 = (bf16[256,2,768]{2,1,0:T(2,128)(2,1)}, bf16[256,2,768]{2,1,0:T(2,128)(2,1)S(1)}, u32[]{:S(2)}) copy-start(bf16[256,2,768]{2,1,0:T(2,128)(2,1)S(1)} %reshape.95) | copy-start | bytes 2359300
  44.7 12.8 %collective-permute-start = (bf16[3,2,512]{0,2,1:T(8,128)(2,1)}, bf16[3,2,512]{0,2,1:T(8,128)(2,1)}, u32[]{:S(2)}, u32[]{:S(2)}) collective-permute-start(bf16[3,2,512]{0,2,1:T(8,128)(2,1)} %copy.69), channel_id=1, source_target_pairs={{0,8},{8,16},{16,24},{24,32},{32,40},{40,48},{48,56},{56,64},{64,7... | collective-permute-start | bytes 18440 | tf_op jit(solution)/shard_map/ppermute | solution.py:18
  65.4 3.2 copy-start.6
  69.4 109.0 %copy-start.10 = (f32[128]{0:T(128)S(1)}, f32[128]{0:T(128)}, u32[]{:S(2)}) copy-start(f32[128]{0:T(128)} %param.20) | copy-start | bytes 1540
  117.2 2.2 copy-start.1
  117.2 2.2 copy-start.2
  117.2 2.9 copy-start.4
  120.8 1.0 copy-start.5
  170.8 2.2 copy-start.1
  170.9 2.2 copy-start.2
  170.9 2.9 copy-start.4
  174.4 1.0 copy-start.5
  177.4 162.8 %all-gather.8.cloned.1.call-start = ((), (), s32[]{:S(2)}) async-start(), calls=%async_computation.3 | async-start | bytes 4325376 | tf_op jit(solution)/shard_map/all_gather | solution.py:133
  178.2 294.6 %reduce-scatter.2.cloned.1.call-start = ((), (), s32[]{:S(2)}) async-start(), calls=%async_computation.2 | async-start | bytes 1179648 | tf_op jit(solution)/shard_map/reduce_scatter | solution.py:159
Sparse Core Ops, SparseCore 0:
  9.2 26.3 all-gather.5
  177.5 80.8 all-gather.9
  261.0 79.1 all-gather.7
  440.2 32.5 reduce-scatter.1
where the time goes:
time: 485 us; the launch traced here: 479 us
  waiting for transfers between devices  217 us (45%)
  other arithmetic  100 us (21%)
  matrix products  80 us (16%)
  local copies, waits for them, and re-layouts  63.3 us (13%)
  between operations  13.4 us (3%)
    another operation x6, other arithmetic, advance(): jax.scipy.linalg.solve_triangular(system, right_side, lower=True, unit_di...  80.4 us
    all_gather x1, waiting for transfers between devices, per_device(): lax.all_gather(local_shift[None].astype(jnp.bfloat16), 'seq', axis=0, til...  76.2 us
    all_gather x1, waiting for transfers between devices, per_device(): lax.all_gather(local_map[None].astype(jnp.bfloat16), 'seq', axis=0, tiled...  75.3 us
    dot_general x32, matrix products, fold_step(): jnp.einsum('hwd,hde->hwe', running, gathered[0][offset], precision=PRECISE)  49.7 us
    dynamic_slice x64, local copies, waits for them, and re-layouts, fold_step(): gathered[1][offset]  35.2 us
    reduce_scatter x1, waiting for transfers between devices, per_device(): lax.psum_scatter(partial_value.astype(jnp.bfloat16), 'head', scatter_dime...  32.7 us
    all_gather x1, waiting for transfers between devices, per_device(): pieces = lax.all_gather(tokens, 'head', axis=1, tiled=True)  26.8 us
  transfers between devices with their start and end apart: 5, of which 5 were waited for; matrix products, arithmetic and copies ran while one was open for 3% of the time, Pallas kernels for 0%

commit v1 on v0

v1 whole, which is shorter than its diff:
```python
import functools

import jax
import jax.numpy as jnp
from jax import lax
from jax.experimental import pallas as pl
from jax.experimental.pallas import tpu as pltpu
from jax.sharding import PartitionSpec as P

F32 = jnp.float32
BF16 = jnp.bfloat16
EPSILON = 1e-06

ROWS = 256
HALF = 128
HEAD = 128
FEATURES = 256
GROUPS = 2
VALUE_HEADS = 4
CONV = 512
GROUP = 768
HALO = 16
NX = 4
NZ = 8
NY = 4

ORDER = ((0, 0), (0, 1), (1, 0), (1, 1), (3, 0), (3, 1), (2, 0), (2, 1))
SLOT = {pair: slot for slot, pair in enumerate(ORDER)}


def matmul(a, b):
    return jnp.dot(a, b, preferred_element_type=F32)


def matmul_t(a, b):
    return lax.dot_general(a, b, (((1,), (1,)), ((), ())), preferred_element_type=F32)


def silu(v):
    return 0.5 * v * (1.0 + jnp.tanh(0.5 * v))


def kernel(
    tokens_hbm,
    in_weight_hbm,
    gate_weight,
    conv_weight,
    decay_scale,
    dt_bias,
    beta_shift,
    norm_gain,
    out_weight_hbm,
    out_ref,
    tok,
    w_in,
    w_out,
    acc,
    ext,
    halo_out,
    halo_in,
    gates,
    qn,
    kn,
    vn,
    maps,
    row_maps,
    row_total,
    all_totals,
    fold_states,
    state_in,
    row_states,
    states,
    loc,
    qeff,
    own,
    sib_out,
    sib_in,
    far_out,
    far_in,
    near_out,
    near_in,
    load_sem,
    win_sem,
    wout_sem,
    tok_send,
    tok_recv,
    halo_sem,
    row_send,
    row_recv,
    tot_send,
    tot_recv,
    fold_send,
    fold_recv,
    back_send,
    back_recv,
    sib_send,
    sib_recv,
    ring_send,
    ring_recv,
):
    seq = lax.axis_index("seq")
    head = lax.axis_index("head")
    z, x = lax.div(seq, NX), lax.rem(seq, NX)
    y, c = lax.div(head, 2), lax.rem(head, 2)

    def head_at(r, other):
        core = c if other == 0 else 1 - c
        return lax.rem(y + r, NY) * 2 + core

    above = (seq, head_at(1, 0))
    below = (seq, head_at(3, 0))
    sibling = (seq, head_at(0, 1))

    def remote(src, dst, send, recv, device):
        return pltpu.make_async_remote_copy(
            src_ref=src,
            dst_ref=dst,
            send_sem=send,
            recv_sem=recv,
            device_id=device,
            device_id_type=pl.DeviceIdType.MESH,
        )

    load_tok = pltpu.make_async_copy(tokens_hbm, tok.at[:, pl.ds(0, FEATURES)], load_sem)
    load_tok.start()
    load_in = []
    for slot, (r, other) in enumerate(ORDER):
        rows = pl.ds(pl.multiple_of(head_at(r, other) * FEATURES, FEATURES), FEATURES)
        copy = pltpu.make_async_copy(
            in_weight_hbm.at[rows], w_in.at[pl.ds(slot * FEATURES, FEATURES)], win_sem.at[slot]
        )
        copy.start()
        load_in.append(copy)
    load_out = []
    for slot, (r, other) in enumerate(ORDER):
        columns = pl.ds(pl.multiple_of(head_at(r, other) * FEATURES, FEATURES), FEATURES)
        copy = pltpu.make_async_copy(out_weight_hbm.at[:, columns], w_out.at[slot], wout_sem.at[slot])
        copy.start()
        load_out.append(copy)

    barrier = pltpu.get_barrier_semaphore()
    next_seq = lax.rem(seq + 1, NX * NZ)
    prev_seq = lax.rem(seq + NX * NZ - 1, NX * NZ)
    partners = [above, below, sibling, (next_seq, head), (prev_seq, head)]
    partners += [(z * NX + lax.rem(x + r, NX), head) for r in range(1, NX)]
    partners += [(lax.rem(z + r, NZ) * NX + x, head) for r in range(1, NZ)]
    for device in partners:
        pl.semaphore_signal(barrier, inc=1, device_id=device, device_id_type=pl.DeviceIdType.MESH)
    pl.semaphore_wait(barrier, len(partners))
    load_tok.wait()

    def tok_part(slot, half):
        return tok.at[pl.ds(half * HALF, HALF), pl.ds(slot * FEATURES, FEATURES)]

    sends = []

    def send_tok(src_slot, dst_slot, half, device):
        copy = remote(
            tok_part(src_slot, half),
            tok_part(dst_slot, half),
            tok_send.at[len(sends)],
            tok_recv.at[2 * dst_slot + half],
            device,
        )
        copy.start()
        sends.append(copy)

    def wait_tok(slot, half):
        remote(
            tok_part(slot, half), tok_part(slot, half), tok_send.at[0], tok_recv.at[2 * slot + half], sibling
        ).wait_recv()

    up, down, far = SLOT[(1, 0)], SLOT[(3, 0)], SLOT[(2, 0)]
    send_tok(0, down, 0, above)
    send_tok(0, up, 1, below)
    send_tok(0, down, 1, above)
    send_tok(0, up, 0, below)
    send_tok(0, 1, 0, sibling)
    send_tok(0, 1, 1, sibling)
    wait_tok(down, 0)
    send_tok(down, far, 0, above)
    wait_tok(up, 1)
    send_tok(up, far, 1, below)
    send_tok(down, down + 1, 0, sibling)
    send_tok(up, up + 1, 1, sibling)

    def project(first, count, start):
        depth = count * FEATURES
        rows = pl.ds(first * FEATURES, depth)

        def tile(j, carry):
            columns = pl.ds(pl.multiple_of(j * 256, 256), 256)
            part = matmul(tok[:, rows], w_in[rows, columns])
            if start:
                acc[:, columns] = part
            else:
                acc[:, columns] += part
            return carry

        lax.fori_loop(0, GROUPS * GROUP // 256, tile, 0)

    wait_tok(1, 0)
    wait_tok(1, 1)
    load_in[0].wait()
    load_in[1].wait()
    project(0, 2, True)
    wait_tok(down, 1)
    send_tok(down, down + 1, 1, sibling)
    wait_tok(up, 0)
    send_tok(up, up + 1, 0, sibling)
    for slot in (up + 1, down + 1):
        wait_tok(slot, 0)
        wait_tok(slot, 1)
    for slot in range(2, 6):
        load_in[slot].wait()
    project(2, 4, False)
    wait_tok(far, 0)
    send_tok(far, far + 1, 0, sibling)
    wait_tok(far, 1)
    send_tok(far, far + 1, 1, sibling)
    wait_tok(far + 1, 0)
    wait_tok(far + 1, 1)
    load_in[6].wait()
    load_in[7].wait()
    project(6, 2, False)
    for copy in sends:
        copy.wait_send()

    for g in range(GROUPS):
        columns = acc[:, g * GROUP : g * GROUP + CONV].astype(BF16)
        halo_out[:, g * CONV : (g + 1) * CONV] = columns[ROWS - HALO :]
        ext[8:, g * CONV : (g + 1) * CONV] = columns.astype(F32)
    send_halo = remote(halo_out, halo_in, halo_sem.at[0], halo_sem.at[1], (next_seq, head))
    send_halo.start()

    gating = jnp.zeros((ROWS, HEAD), F32)
    for slot, (r, other) in enumerate(ORDER):
        rows = pl.ds(pl.multiple_of(head_at(r, other) * FEATURES, FEATURES), FEATURES)
        weight = gate_weight[rows, :]
        weight = jnp.concatenate([weight, jnp.zeros((FEATURES, HEAD - weight.shape[1]), BF16)], 1)
        gating = gating + matmul(tok[:, slot * FEATURES : (slot + 1) * FEATURES], weight)
    lane = lax.broadcasted_iota(jnp.int32, (1, HEAD), 1)
    shift = jnp.zeros((1, HEAD), F32)
    bias = jnp.zeros((1, HEAD), F32)
    scale = jnp.zeros((1, HEAD), F32)
    for h in range(VALUE_HEADS):
        g, r = divmod(h, 2)
        shift = jnp.where(lane == 4 * g + r, beta_shift[h], shift)
        bias = jnp.where(lane == 4 * g + 2 + r, dt_bias[h], bias)
        scale = jnp.where(lane == 4 * g + 2 + r, decay_scale[h], scale)
    strength = jax.nn.sigmoid(gating - shift)
    shifted = gating + bias
    softplus = jnp.maximum(shifted, 0.0) + jnp.log1p(jnp.exp(-jnp.abs(shifted)))
    log_gate = -scale * softplus
    row_id = lax.broadcasted_iota(jnp.int32, (ROWS, ROWS), 0)
    col_id = lax.broadcasted_iota(jnp.int32, (ROWS, ROWS), 1)
    ones = jnp.where(col_id <= row_id, 1.0, 0.0).astype(BF16)
    cumulative = jnp.zeros((ROWS, HEAD), F32)
    rest = log_gate
    for _ in range(3):
        piece = rest.astype(BF16)
        cumulative = cumulative + matmul(ones, piece)
        rest = rest - piece.astype(F32)
    cumulative_t = jnp.transpose(cumulative)
    gates[0] = strength
    gates[1] = cumulative

    def convolve(first, count):
        for g in range(GROUPS):
            for block in range(CONV // HEAD):
                lanes = pl.ds(g * CONV + block * HEAD, HEAD)
                total = jnp.zeros((count, HEAD), F32)
                for tap in range(4):
                    weight = conv_weight[tap, g : g + 1, block * HEAD : (block + 1) * HEAD].astype(F32)
                    total = total + weight * ext[pl.ds(first + 5 + tap, count), lanes]
                value = silu(total)
                rows = pl.ds(first, count)
                if block < 2:
                    norm = lax.rsqrt(jnp.sum(value * value, -1, keepdims=True) + EPSILON)
                    if block == 0:
                        qn[g, rows, :] = (value * (norm * HEAD**-0.5)).astype(BF16)
                    else:
                        kn[g, rows, :] = (value * norm).astype(BF16)
                else:
                    vn[2 * g + block - 2, rows, :] = value.astype(BF16)

    convolve(HALO, ROWS - HALO)
    send_halo.wait_recv()
    before = jnp.where(seq > 0, halo_in[...].astype(F32), 0.0)
    ext[0:8, :] = before[HALO - 8 :]
    convolve(0, HALO)

    row = lax.broadcasted_iota(jnp.int32, (HEAD, HEAD), 0)
    col = lax.broadcasted_iota(jnp.int32, (HEAD, HEAD), 1)
    on_lower = col <= row
    below_diag = col < row
    unit = jnp.where(col == row, 1.0, 0.0)
    unit_b = unit.astype(BF16)
    masks = []
    b = 1
    while b < HEAD:
        keep = (lax.div(row, 2 * b) == lax.div(col, 2 * b)) & (lax.div(row, b) != lax.div(col, b)) & below_diag
        masks.append(jnp.where(keep, 1.0, 0.0).astype(BF16))
        b *= 2

    parts = [pl.ds(0, HEAD), pl.ds(HEAD, HEAD)]
    inner = []
    for g in range(GROUPS):
        inner.append(matmul_t(jnp.concatenate([kn[g], qn[g]], 0), kn[g]))
    systems, scores = [], []
    for h in range(VALUE_HEADS):
        g, r = divmod(h, 2)
        lane_b, lane_c = 4 * g + r, 4 * g + 2 + r
        beta = gates[0][:, lane_b : lane_b + 1]
        cum = gates[1][:, lane_c : lane_c + 1]
        cum_t = cumulative_t[lane_c : lane_c + 1, :]
        system, score = {}, {}
        for i, j in ((0, 0), (1, 0), (1, 1)):
            ri, cj = slice(i * HEAD, (i + 1) * HEAD), slice(j * HEAD, (j + 1) * HEAD)
            gap = cum[ri] - cum_t[:, cj]
            if i == j:
                ratio = jnp.where(on_lower, jnp.exp(jnp.where(on_lower, gap, 0.0)), 0.0)
            else:
                ratio = jnp.exp(gap)
            system[i, j] = (beta[ri] * ratio * inner[g][ri, cj]).astype(BF16)
            score[i, j] = (ratio * inner[g][ROWS + i * HEAD : ROWS + (i + 1) * HEAD, cj]).astype(BF16)
        systems.append(system)
        scores.append(score)
    inverses = {(h, i): unit_b - masks[0] * systems[h][i, i] for h in range(VALUE_HEADS) for i in range(2)}
    for mask in masks[1:]:
        halves = {
            key: matmul(mask * systems[key[0]][key[1], key[1]], inverses[key]).astype(BF16) for key in inverses
        }
        inverses = {key: inverses[key] - matmul(inverses[key], halves[key]).astype(BF16) for key in inverses}

    solved = []
    for h in range(VALUE_HEADS):
        g, r = divmod(h, 2)
        lane_b, lane_c = 4 * g + r, 4 * g + 2 + r
        beta = gates[0][:, lane_b : lane_b + 1]
        cum = gates[1][:, lane_c : lane_c + 1]
        right = jnp.concatenate(
            [beta * jnp.exp(cum) * kn[g].astype(F32), beta * vn[h].astype(F32)], 1
        )
        first = matmul(inverses[h, 0], right[:HEAD].astype(BF16)).astype(BF16)
        second = right[HEAD:] - matmul(systems[h][1, 0], first)
        second = matmul(inverses[h, 1], second.astype(BF16)).astype(BF16)
        both = jnp.concatenate([first, second], 0)
        solved.append(both)
        last = cum[ROWS - 1 :, :]
        end_keys = (jnp.exp(last - cum) * kn[g].astype(F32)).astype(BF16)
        grown = lax.dot_general(end_keys, both, (((0,), (0,)), ((), ())), preferred_element_type=F32)
        change = (jnp.exp(last) - 1.0) * unit - grown[:, :HEAD]
        maps[h] = jnp.concatenate([change, grown[:, HEAD:]], 1).astype(BF16)

    def row_device(r):
        return (z * NX + lax.rem(x + r, NX), head)

    row_copies = []
    for r in range(1, NX):
        there = lax.rem(x + r, NX)
        copy = remote(maps.at[there], row_maps.at[x], row_send.at[r - 1], row_recv.at[r - 1], row_device(r))
        copy.start()
        row_copies.append(copy)
    row_maps[pl.ds(x, 1)] = maps[pl.ds(x, 1)]

    for h in range(VALUE_HEADS):
        g, r = divmod(h, 2)
        lane_c = 4 * g + 2 + r
        cum = gates[1][:, lane_c : lane_c + 1]
        top = matmul(scores[h][0, 0], solved[h][:HEAD])
        low = matmul(jnp.concatenate([scores[h][1, 0], scores[h][1, 1]], 1), solved[h])
        out = jnp.concatenate([top, low], 0)
        qeff[h] = (jnp.exp(cum) * qn[g].astype(F32) - out[:, :HEAD]).astype(BF16)
        loc[h] = out[:, HEAD:]

    for r in range(1, NX):
        here = lax.rem(x + NX - r, NX)
        remote(maps.at[0], row_maps.at[here], row_send.at[r - 1], row_recv.at[r - 1], row_device(r)).wait_recv()

    prefix = [row_maps[0].astype(F32)]
    for i in range(1, NX):
        previous = prefix[-1]
        change = row_maps[i]
        prefix.append(previous + change.astype(F32) + matmul(change[:, :HEAD], previous.astype(BF16)))
    row_total[...] = prefix[-1].astype(BF16)

    center = 3 + 4 * c
    is_center = z == center

    def column_device(there):
        return (there * NX + x, head)

    @pl.when(jnp.logical_and(jnp.logical_not(is_center), z != NZ - 1))
    def _():
        remote(
            row_total, all_totals.at[z], tot_send.at[0], tot_recv.at[z], column_device(center)
        ).start()

    @pl.when(is_center)
    def _():
        all_totals[pl.ds(z, 1)] = row_total[...][None]
        fold = jnp.zeros((HEAD, HEAD), F32)
        for k in range(NZ - 1):
            arrival = remote(
                row_total, all_totals.at[k], tot_send.at[0], tot_recv.at[k], column_device(0 * z)
            )
            if k == 3:
                pl.when(c == 1)(arrival.wait_recv)
            else:
                arrival.wait_recv()
            total = all_totals[k]
            if k == 0:
                fold = total[:, HEAD:].astype(F32)
            else:
                fold = (
                    fold + total[:, HEAD:].astype(F32) + matmul(total[:, :HEAD], fold.astype(BF16))
                )
            fold_states[k + 1] = fold.astype(BF16)
            leave = remote(
                fold_states.at[k + 1], state_in, fold_send.at[k + 1], fold_recv, column_device(k + 1)
            )
            if k + 1 == 3:
                pl.when(c == 1)(leave.start)
            elif k + 1 == 7:
                pl.when(c == 0)(leave.start)
            else:
                leave.start()
        state_in[...] = fold_states[pl.ds(z, 1)][0]

    @pl.when(z == 0)
    def _():
        state_in[...] = jnp.zeros_like(state_in)

    @pl.when(jnp.logical_and(jnp.logical_not(is_center), z != 0))
    def _():
        remote(
            fold_states.at[0], state_in, fold_send.at[0], fold_recv, column_device(center)
        ).wait_recv()

    state = state_in[...]
    row_states[0] = state
    for i in range(1, NX):
        before_i = prefix[i - 1]
        row_states[i] = (
            state.astype(F32) + before_i[:, HEAD:] + matmul(before_i[:, :HEAD].astype(BF16), state)
        ).astype(BF16)
    back_copies = []
    for r in range(1, NX):
        there = lax.rem(x + r, NX)
        copy = remote(row_states.at[there], states.at[x], back_send.at[r - 1], back_recv.at[r - 1], row_device(r))
        copy.start()
        back_copies.append(copy)
    states[pl.ds(x, 1)] = row_states[pl.ds(x, 1)]
    for r in range(1, NX):
        here = lax.rem(x + NX - r, NX)
        remote(
            row_states.at[0], states.at[here], back_send.at[r - 1], back_recv.at[r - 1], row_device(r)
        ).wait_recv()

    gain = norm_gain[...].reshape(1, HEAD)
    hidden = []
    for h in range(VALUE_HEADS):
        g, r = divmod(h, 2)
        first = g * GROUP + CONV + r * HEAD
        attended = loc[h] + matmul(qeff[h], states[h])
        back = lax.rsqrt(jnp.mean(attended * attended, -1, keepdims=True) + EPSILON)
        gate = acc[:, first : first + HEAD].astype(BF16).astype(F32)
        hidden.append((attended * back * gain * silu(gate)).astype(BF16))
    hidden = jnp.concatenate(hidden, 1)

    for r in (2, 1, 3, 0):
        slot = SLOT[(r, 1)]
        load_out[slot].wait()
        sib_out[r] = matmul(hidden, w_out[slot]).astype(BF16)
        remote(sib_out.at[r], sib_in.at[r], sib_send.at[r], sib_recv.at[r], sibling).start()
    for r in (2, 1, 3, 0):
        slot = SLOT[(r, 0)]
        load_out[slot].wait()
        own[r] = matmul(hidden, w_out[slot])

    def wait_sibling(r):
        remote(sib_out.at[r], sib_in.at[r], sib_send.at[r], sib_recv.at[r], sibling).wait_recv()

    top, low = pl.ds(0, HALF), pl.ds(HALF, HALF)
    far_up = remote(far_out.at[top], far_in.at[top], ring_send.at[0], ring_recv.at[0], above)
    far_down = remote(far_out.at[low], far_in.at[low], ring_send.at[1], ring_recv.at[1], below)
    up_low = remote(near_out.at[0, low], near_in.at[0, low], ring_send.at[2], ring_recv.at[2], above)
    down_top = remote(near_out.at[1, top], near_in.at[1, top], ring_send.at[3], ring_recv.at[3], below)
    up_top = remote(near_out.at[0, top], near_in.at[0, top], ring_send.at[4], ring_recv.at[4], above)
    down_low = remote(near_out.at[1, low], near_in.at[1, low], ring_send.at[5], ring_recv.at[5], below)
    wait_sibling(2)
    far_out[...] = (own[2] + sib_in[2].astype(F32)).astype(BF16)
    far_up.start()
    far_down.start()
    wait_sibling(1)
    near_out[0, HALF:] = (own[1, HALF:] + sib_in[1, HALF:].astype(F32)).astype(BF16)
    up_low.start()
    wait_sibling(3)
    near_out[1, :HALF] = (own[3, :HALF] + sib_in[3, :HALF].astype(F32)).astype(BF16)
    down_top.start()
    far_up.wait_recv()
    near_out[0, :HALF] = (
        own[1, :HALF] + sib_in[1, :HALF].astype(F32) + far_in[:HALF].astype(F32)
    ).astype(BF16)
    up_top.start()
    far_down.wait_recv()
    near_out[1, HALF:] = (
        own[3, HALF:] + sib_in[3, HALF:].astype(F32) + far_in[HALF:].astype(F32)
    ).astype(BF16)
    down_low.start()
    wait_sibling(0)
    mine = own[0] + sib_in[0].astype(F32)
    for copy in (up_low, down_top, up_top, down_low):
        copy.wait_recv()
    out_ref[...] = (mine + near_in[0].astype(F32) + near_in[1].astype(F32)).astype(BF16)

    send_halo.wait_send()
    for copy in row_copies + back_copies:
        copy.wait_send()

    @pl.when(jnp.logical_and(jnp.logical_not(is_center), z != NZ - 1))
    def _():
        remote(
            row_total, all_totals.at[z], tot_send.at[0], tot_recv.at[z], column_device(center)
        ).wait_send()

    @pl.when(is_center)
    def _():
        for k in range(1, NZ):
            leave = remote(fold_states.at[k], state_in, fold_send.at[k], fold_recv, column_device(k))
            if k == 3:
                pl.when(c == 1)(leave.wait_send)
            elif k == 7:
                pl.when(c == 0)(leave.wait_send)
            else:
                leave.wait_send()

    for r in range(NY):
        remote(sib_out.at[r], sib_in.at[r], sib_send.at[r], sib_recv.at[r], sibling).wait_send()
    for copy in (far_up, far_down, up_low, down_top, up_top, down_low):
        copy.wait_send()


def per_device(*args):
    anywhere = pl.BlockSpec(memory_space=pl.ANY)
    vmem = pl.BlockSpec(memory_space=pltpu.VMEM)
    smem = pl.BlockSpec(memory_space=pltpu.SMEM)
    dma = pltpu.SemaphoreType.DMA
    return pl.pallas_call(
        kernel,
        out_shape=jax.ShapeDtypeStruct((ROWS, FEATURES), BF16),
        in_specs=[anywhere, anywhere, vmem, vmem, smem, smem, smem, vmem, anywhere],
        out_specs=vmem,
        scratch_shapes=[
            pltpu.VMEM((ROWS, 8 * FEATURES), BF16),
            pltpu.VMEM((8 * FEATURES, GROUPS * GROUP), BF16),
            pltpu.VMEM((8, VALUE_HEADS * HEAD, FEATURES), BF16),
            pltpu.VMEM((ROWS, GROUPS * GROUP), F32),
            pltpu.VMEM((8 + ROWS, GROUPS * CONV), F32),
            pltpu.VMEM((HALO, GROUPS * CONV), BF16),
            pltpu.VMEM((HALO, GROUPS * CONV), BF16),
            pltpu.VMEM((2, ROWS, HEAD), F32),
            pltpu.VMEM((GROUPS, ROWS, HEAD), BF16),
            pltpu.VMEM((GROUPS, ROWS, HEAD), BF16),
            pltpu.VMEM((VALUE_HEADS, ROWS, HEAD), BF16),
            pltpu.VMEM((VALUE_HEADS, HEAD, 2 * HEAD), BF16),
            pltpu.VMEM((NX, HEAD, 2 * HEAD), BF16),
            pltpu.VMEM((HEAD, 2 * HEAD), BF16),
            pltpu.VMEM((NZ, HEAD, 2 * HEAD), BF16),
            pltpu.VMEM((NZ, HEAD, HEAD), BF16),
            pltpu.VMEM((HEAD, HEAD), BF16),
            pltpu.VMEM((NX, HEAD, HEAD), BF16),
            pltpu.VMEM((VALUE_HEADS, HEAD, HEAD), BF16),
            pltpu.VMEM((VALUE_HEADS, ROWS, HEAD), F32),
            pltpu.VMEM((VALUE_HEADS, ROWS, HEAD), BF16),
            pltpu.VMEM((NY, ROWS, FEATURES), F32),
            pltpu.VMEM((NY, ROWS, FEATURES), BF16),
            pltpu.VMEM((NY, ROWS, FEATURES), BF16),
            pltpu.VMEM((ROWS, FEATURES), BF16),
            pltpu.VMEM((ROWS, FEATURES), BF16),
            pltpu.VMEM((2, ROWS, FEATURES), BF16),
            pltpu.VMEM((2, ROWS, FEATURES), BF16),
            dma,
            dma((8,)),
            dma((8,)),
            dma((14,)),
            dma((16,)),
            dma((2,)),
            dma((NX - 1,)),
            dma((NX - 1,)),
            dma((1,)),
            dma((NZ,)),
            dma((NZ,)),
            dma,
            dma((NX - 1,)),
            dma((NX - 1,)),
            dma((NY,)),
            dma((NY,)),
            dma((6,)),
            dma((6,)),
        ],
        compiler_params=pltpu.CompilerParams(
            collective_id=0, has_side_effects=True, vmem_limit_bytes=48 * 1024 * 1024
        ),
    )(*args)


def solution(mesh):
    in_specs = (
        P("seq", "head"),
        P(None, "head"),
        P(None, "head"),
        P(None, "head", None),
        P("head"),
        P("head"),
        P("head"),
        P(),
        P("head", None),
    )
    out_specs = P("seq", "head")
    return jax.shard_map(
        per_device, mesh=mesh, in_specs=in_specs, out_specs=out_specs, check_vma=False
    )
```

time: 485 us -> 63.5 us (0.13); the launches traced: 479 us -> 62.8 us
  waiting for transfers between devices: 217 us -> 0 us
  other arithmetic: 100 us -> 0 us
  matrix products: 80 us -> 0 us
  local copies, waits for them, and re-layouts: 63.3 us -> 7.49 us
  Pallas kernels: 0 us -> 55.3 us
  between operations: 13.4 us -> 0.03 us
    all_gather x3 -> x0, waiting for transfers between devices: 178 us -> none  [the longest x1 76.2 us: per_device(): lax.all_gather(local_shift[None].astype(jnp.bfloat16), 'seq', axis=0, til...]
    another operation x7 -> x0, other arithmetic: 80.5 us -> none  [the longest x6 80.4 us: advance(): jax.scipy.linalg.solve_triangular(system, right_side, lower=True, unit_di...]
    dot_general x50 -> x0, matrix products: 78.8 us -> none  [the longest x32 49.7 us: fold_step(): jnp.einsum('hwd,hde->hwe', running, gathered[0][offset], precision=PRECISE)]
    pallas_call x0 -> x1, Pallas kernels: none -> 55.3 us  [per_device(): pl.pallas_call(kernel, out_shape=jax.ShapeDtypeStruct((ROWS, FEATURES), B...]
    dynamic_slice x70 -> x0, local copies, waits for them, and re-layouts: 40.9 us -> none  [the longest x64 35.2 us: fold_step(): gathered[1][offset]]
    reduce_scatter x1 -> x0, waiting for transfers between devices: 32.7 us -> none  [per_device(): lax.psum_scatter(partial_value.astype(jnp.bfloat16), 'head', scatter_dime...]
    convert_element_type x8 -> x0, other arithmetic: 16.3 us -> none  [the longest x1 6.49 us: per_device(): lax.all_gather(local_shift[None].astype(jnp.bfloat16), 'seq', axis=0, til...]
  transfers between devices with their start and end apart: 5 -> 0, of which waited for: 5 -> 0; matrix products, arithmetic and copies ran while one was open for 3% -> 0% of each run, Pallas kernels for 0% -> 0%
where the time goes in v1:
time: 63.5 us; the launch traced here: 62.8 us
  Pallas kernels  55.3 us (87%)
  local copies, waits for them, and re-layouts  7.49 us (12%)
    pallas_call x1, Pallas kernels, per_device(): pl.pallas_call(kernel, out_shape=jax.ShapeDtypeStruct((ROWS, FEATURES), B...  55.3 us
    unnamed x16, local copies, waits for them, and re-layouts  7.49 us

profile of v1, /device:TPU:224, one launch (start us, length us, event | category | flops | bytes accessed | tf_op | source)
XLA Modules:
  0.0 62.8 jit_solution(5388225815217467522)
XLA Ops:
  0.0 1.0 %copy.10.gate_weight = bf16[2048,8]{1,0:T(8,128)(2,1)S(1)} copy(bf16[2048,8]{0,1:T(8,128)(2,1)} %param.11) | data formatting | bytes 65536 | tf_op args[2]
  1.0 0.0 copy-start
  1.0 1.6 %copy-done = bf16[512,2048]{1,0:T(8,128)(2,1)S(1)} copy-done((bf16[512,2048]{1,0:T(8,128)(2,1)S(1)}, bf16[512,2048]{1,0:T(8,128)(2,1)}, u32[]{:S(2)}) %copy-start) | copy-done | bytes 2097176
  2.6 0.0 copy-start.1
  2.6 0.9 %copy-done.1 = bf16[256,256]{1,0:T(8,128)(2,1)S(1)} copy-done((bf16[256,256]{1,0:T(8,128)(2,1)S(1)}, bf16[256,256]{1,0:T(8,128)(2,1)}, u32[]{:S(2)}) %copy-start.1) | copy-done | bytes 131096
  3.5 0.0 copy-start.2
  3.5 0.7 %copy-done.2 = bf16[4,2,512]{2,1,0:T(2,128)(2,1)S(1)} copy-done((bf16[4,2,512]{2,1,0:T(2,128)(2,1)S(1)}, bf16[4,2,512]{2,1,0:T(2,128)(2,1)}, u32[]{:S(2)}) %copy-start.2) | copy-done | bytes 8216
  4.2 0.0 copy-start.3
  4.2 0.7 %copy-done.3 = f32[4]{0:T(128)S(1)} copy-done((f32[4]{0:T(128)S(1)}, f32[4]{0:T(128)}, u32[]{:S(2)}) %copy-start.3) | copy-done | bytes 40
  4.9 0.0 copy-start.4
  4.9 0.7 %copy-done.4 = f32[4]{0:T(128)S(1)} copy-done((f32[4]{0:T(128)S(1)}, f32[4]{0:T(128)}, u32[]{:S(2)}) %copy-start.4) | copy-done | bytes 40
  5.5 0.0 copy-start.5
  5.5 0.7 %copy-done.5 = f32[4]{0:T(128)S(1)} copy-done((f32[4]{0:T(128)S(1)}, f32[4]{0:T(128)}, u32[]{:S(2)}) %copy-start.5) | copy-done | bytes 40
  6.2 0.0 copy-start.6
  6.2 0.7 %copy-done.6 = f32[128]{0:T(128)S(1)} copy-done((f32[128]{0:T(128)S(1)}, f32[128]{0:T(128)}, u32[]{:S(2)}) %copy-start.6) | copy-done | bytes 536
  6.9 55.3 %shard_map.91 = bf16[256,256]{1,0:T(8,128)(2,1)S(1)} custom-call(bf16[256,256]{1,0:T(8,128)(2,1)S(1)} %copy-done.1, bf16[2048,1536]{1,0:T(8,128)(2,1)} %in_weight_hbm.1, bf16[2048,8]{1,0:T(8,128)(2,1)S(1)} %copy.10.gate_weight, bf16[4,2,512]{2,1,0:T(2,128)(2,1)S(1)} %copy-done.2, f32[4]{0:T(128)S(1)} %copy-done.3, f32[4]{0:T(128)S(1)} %copy-done.4, ...), custom_call_target="tpu_custom_call" | custom-call | tf_op jit(solution)/shard_map/pallas_call | solution.py:550
  62.2 0.7 %copy.12 = bf16[256,256]{1,0:T(8,128)(2,1)} copy(bf16[256,256]{1,0:T(8,128)(2,1)S(1)} %shard_map.91) | data formatting | bytes 262144
Async XLA Ops:
  1.0 1.6 %copy-start = (bf16[512,2048]{1,0:T(8,128)(2,1)S(1)}, bf16[512,2048]{1,0:T(8,128)(2,1)}, u32[]{:S(2)}) copy-start(bf16[512,2048]{1,0:T(8,128)(2,1)} %out_weight_hbm.1) | copy-start | bytes 6291460
  2.6 0.9 %copy-start.1 = (bf16[256,256]{1,0:T(8,128)(2,1)S(1)}, bf16[256,256]{1,0:T(8,128)(2,1)}, u32[]{:S(2)}) copy-start(bf16[256,256]{1,0:T(8,128)(2,1)} %tokens_hbm.1) | copy-start | bytes 393220
  3.5 0.7 %copy-start.2 = (bf16[4,2,512]{2,1,0:T(2,128)(2,1)S(1)}, bf16[4,2,512]{2,1,0:T(2,128)(2,1)}, u32[]{:S(2)}) copy-start(bf16[4,2,512]{2,1,0:T(2,128)(2,1)} %conv_weight.1) | copy-start | bytes 24580
  4.2 0.7 %copy-start.3 = (f32[4]{0:T(128)S(1)}, f32[4]{0:T(128)}, u32[]{:S(2)}) copy-start(f32[4]{0:T(128)} %decay_scale.1) | copy-start | bytes 52
  4.9 0.7 %copy-start.4 = (f32[4]{0:T(128)S(1)}, f32[4]{0:T(128)}, u32[]{:S(2)}) copy-start(f32[4]{0:T(128)} %dt_bias.1) | copy-start | bytes 52
  5.5 0.7 %copy-start.5 = (f32[4]{0:T(128)S(1)}, f32[4]{0:T(128)}, u32[]{:S(2)}) copy-start(f32[4]{0:T(128)} %beta_shift.1) | copy-start | bytes 52
  6.2 0.7 %copy-start.6 = (f32[128]{0:T(128)S(1)}, f32[128]{0:T(128)}, u32[]{:S(2)}) copy-start(f32[128]{0:T(128)} %norm_gain.1) | copy-start | bytes 1540

commit v2 on v1

v2 whole, which is shorter than its diff:
```python
import functools

import jax
import jax.numpy as jnp
from jax import lax
from jax.experimental import pallas as pl
from jax.experimental.pallas import tpu as pltpu
from jax.sharding import PartitionSpec as P

F32 = jnp.float32
BF16 = jnp.bfloat16
EPSILON = 1e-06

ROWS = 256
HEAD = 128
FEATURES = 256
GROUPS = 2
VALUE_HEADS = 4
TILES = 6
CONV = 512
GROUP = 768
HALO = 16
NX = 4
NZ = 8
QUAD = 4
NY = 4

ORDER = ((0, 0), (0, 1), (1, 0), (1, 1), (3, 0), (3, 1), (2, 0), (2, 1))
SLOT = {pair: slot for slot, pair in enumerate(ORDER)}


def matmul(a, b):
    return jnp.dot(a, b, preferred_element_type=F32)


def matmul_t(a, b):
    return lax.dot_general(a, b, (((1,), (1,)), ((), ())), preferred_element_type=F32)


def silu(v):
    return 0.5 * v * (1.0 + jnp.tanh(0.5 * v))


def kernel(
    tokens_hbm,
    in_weight_hbm,
    gate_weight_hbm,
    conv_weight_hbm,
    decay_scale_hbm,
    dt_bias_hbm,
    beta_shift_hbm,
    norm_gain_hbm,
    out_weight_hbm,
    out_ref,
    gate_weight,
    conv_weight,
    decay_scale,
    dt_bias,
    beta_shift,
    norm_gain,
    tok,
    w_in,
    w_out,
    acc,
    ext,
    halo_out,
    halo_in,
    gates,
    qn,
    kn,
    vn,
    maps,
    row_maps,
    row_total,
    totals_in,
    state_in,
    state_out,
    state_before,
    out_gate,
    row_states,
    states,
    loc,
    qeff,
    own,
    sib_out,
    sib_in,
    ring_out,
    ring_in,
    load_sem,
    small_sem,
    win_sem,
    wout_sem,
    tok_send,
    tok_recv,
    halo_sem,
    row_send,
    row_recv,
    total_send,
    total_recv,
    state_send,
    state_recv,
    ready_sem,
    halo_ready_sem,
    back_send,
    back_recv,
    sib_send,
    sib_recv,
    ring_send,
    ring_recv,
):
    seq = lax.axis_index("seq")
    head = lax.axis_index("head")
    z, x = lax.div(seq, NX), lax.rem(seq, NX)
    y, c = lax.div(head, 2), lax.rem(head, 2)

    def head_at(r, other):
        core = c if other == 0 else 1 - c
        return lax.rem(y + r, NY) * 2 + core

    above = (seq, head_at(1, 0))
    below = (seq, head_at(3, 0))
    across = (seq, head_at(2, 0))
    sibling = (seq, head_at(0, 1))

    def remote(src, dst, send, recv, device):
        return pltpu.make_async_remote_copy(
            src_ref=src,
            dst_ref=dst,
            send_sem=send,
            recv_sem=recv,
            device_id=device,
            device_id_type=pl.DeviceIdType.MESH,
        )

    load_tok = pltpu.make_async_copy(tokens_hbm, tok.at[0], load_sem)
    load_tok.start()
    load_in = []
    for slot, (r, other) in enumerate(ORDER):
        rows = pl.ds(pl.multiple_of(head_at(r, other) * FEATURES, FEATURES), FEATURES)
        copy = pltpu.make_async_copy(
            in_weight_hbm.at[rows], w_in.at[pl.ds(slot * FEATURES, FEATURES)], win_sem.at[slot]
        )
        copy.start()
        load_in.append(copy)
    load_out = []
    for slot, (r, other) in enumerate(ORDER):
        columns = pl.ds(pl.multiple_of(head_at(r, other) * FEATURES, FEATURES), FEATURES)
        copy = pltpu.make_async_copy(out_weight_hbm.at[:, columns], w_out.at[slot], wout_sem.at[slot])
        copy.start()
        load_out.append(copy)

    load_small = []
    for i, (source, target) in enumerate(
        (
            (gate_weight_hbm, gate_weight),
            (conv_weight_hbm, conv_weight),
            (decay_scale_hbm, decay_scale),
            (dt_bias_hbm, dt_bias),
            (beta_shift_hbm, beta_shift),
            (norm_gain_hbm, norm_gain),
        )
    ):
        copy = pltpu.make_async_copy(source, target, small_sem.at[i])
        copy.start()
        load_small.append(copy)

    barrier = pltpu.get_barrier_semaphore()
    def row_device(r):
        return (z * NX + lax.rem(x + r, NX), head)

    def column_device(there):
        return (there * NX + x, head)

    def signal(semaphore, device):
        pl.semaphore_signal(semaphore, inc=1, device_id=device, device_id_type=pl.DeviceIdType.MESH)

    place = lax.rem(z, QUAD)
    upper = z >= QUAD
    base_row = z == QUAD - 1
    last_x = x == NX - 1
    not_top = z < NZ - 1
    next_row = ((z + 1) * NX, head)
    for device in [above, below, across, sibling] + [row_device(r) for r in range(1, NX)]:
        signal(barrier, device)

    for d in range(1, QUAD):
        pl.when(place + d < QUAD)(functools.partial(signal, barrier, column_device(z + d)))
    for d in range(1, QUAD + 1):
        pl.when(base_row)(functools.partial(signal, barrier, column_device(z + d)))

    @pl.when(jnp.logical_and(last_x, not_top))
    def _():
        signal(barrier, next_row)

    greeted = 7 + place + jnp.where(upper, 1, 0)
    greeted = greeted + jnp.where(jnp.logical_and(x == 0, z > 0), 1, 0)
    pl.semaphore_wait(barrier, greeted)

    for d in range(1, QUAD):
        pl.when(place >= d)(functools.partial(signal, ready_sem, column_device(z - d)))
    pl.when(upper)(functools.partial(signal, ready_sem, column_device(QUAD - 1)))

    @pl.when(jnp.logical_and(x == 0, z > 0))
    def _():
        signal(halo_ready_sem, ((z - 1) * NX + NX - 1, head))

    load_tok.wait()

    pending = []

    def finish():
        for wait in pending:
            wait()

    sends = []

    def send_tok(source, target, device):
        copy = remote(tok.at[source], tok.at[target], tok_send.at[len(sends)], tok_recv.at[target], device)
        copy.start()
        sends.append(copy)

    def wait_tok(slot):
        remote(tok.at[slot], tok.at[slot], tok_send.at[0], tok_recv.at[slot], sibling).wait_recv()

    up, down, far = SLOT[(1, 0)], SLOT[(3, 0)], SLOT[(2, 0)]
    send_tok(0, down, above)
    send_tok(0, up, below)
    send_tok(0, 1, sibling)
    send_tok(0, far, across)

    def tokens_of(first, count):
        return jnp.concatenate([tok[slot] for slot in range(first, first + count)], 1)

    def project(first, count, start):
        rows = pl.ds(first * FEATURES, count * FEATURES)

        def tile(j, carry):
            columns = pl.ds(pl.multiple_of(j * 256, 256), 256)
            part = matmul(tokens_of(first, count), w_in[rows, columns])
            if start:
                acc[j] = part
            else:
                acc[j] += part
            return carry

        lax.fori_loop(0, TILES, tile, 0)

    wait_tok(1)
    load_in[0].wait()
    load_in[1].wait()
    project(0, 2, True)
    for slot in (up, down):
        wait_tok(slot)
        send_tok(slot, slot + 1, sibling)
    for slot in range(2, 6):
        load_in[slot].wait()
    wait_tok(up + 1)
    wait_tok(down + 1)
    project(2, 4, False)
    wait_tok(far)
    send_tok(far, far + 1, sibling)
    wait_tok(far + 1)
    load_in[6].wait()
    load_in[7].wait()
    pending.extend(copy.wait_send for copy in sends)

    for g in range(GROUPS):
        for i in range(2):
            j = 3 * g + i
            weight = w_in[6 * FEATURES :, j * 256 : (j + 1) * 256]
            part = (acc[j] + matmul(tokens_of(6, 2), weight)).astype(BF16)
            first = 4 * g + 2 * i
            for block in range(2):
                columns = part[:, block * HEAD : (block + 1) * HEAD]
                halo_out[:, (first + block) * HEAD : (first + block + 1) * HEAD] = columns[ROWS - HALO :]
                ext[first + block, 8:, :] = columns.astype(F32)

    next_seq = lax.rem(seq + 1, NX * NZ)
    send_halo = remote(halo_out, halo_in, halo_sem.at[0], halo_sem.at[1], (next_seq, head))

    @pl.when(jnp.logical_and(last_x, not_top))
    def _():
        pl.semaphore_wait(halo_ready_sem, 1)

    pl.when(seq < NX * NZ - 1)(send_halo.start)
    pending.append(lambda: pl.when(seq < NX * NZ - 1)(send_halo.wait_send))

    for copy in load_small:
        copy.wait()
    gating = jnp.zeros((ROWS, HEAD), F32)
    for slot, (r, other) in enumerate(ORDER):
        columns = pl.ds(pl.multiple_of(head_at(r, other) * FEATURES, FEATURES), FEATURES)
        weight = gate_weight[:, columns]
        weight = jnp.concatenate([weight, jnp.zeros((HEAD - weight.shape[0], FEATURES), BF16)], 0)
        gating = gating + matmul_t(tok[slot], weight)
    lane = lax.broadcasted_iota(jnp.int32, (1, HEAD), 1)
    shift = jnp.zeros((1, HEAD), F32)
    bias = jnp.zeros((1, HEAD), F32)
    scale = jnp.zeros((1, HEAD), F32)
    for h in range(VALUE_HEADS):
        g, r = divmod(h, 2)
        shift = jnp.where(lane == 4 * g + r, beta_shift[h], shift)
        bias = jnp.where(lane == 4 * g + 2 + r, dt_bias[h], bias)
        scale = jnp.where(lane == 4 * g + 2 + r, decay_scale[h], scale)
    strength = jax.nn.sigmoid(gating - shift)
    shifted = gating + bias
    softplus = jnp.maximum(shifted, 0.0) + jnp.log1p(jnp.exp(-jnp.abs(shifted)))
    log_gate = -scale * softplus
    row_id = lax.broadcasted_iota(jnp.int32, (ROWS, ROWS), 0)
    col_id = lax.broadcasted_iota(jnp.int32, (ROWS, ROWS), 1)
    ones = jnp.where(col_id <= row_id, 1.0, 0.0).astype(BF16)
    cumulative = jnp.zeros((ROWS, HEAD), F32)
    rest = log_gate
    for _ in range(3):
        piece = rest.astype(BF16)
        cumulative = cumulative + matmul(ones, piece)
        rest = rest - piece.astype(F32)
    cumulative_t = jnp.transpose(cumulative)
    gates[0] = strength
    gates[1] = cumulative

    def convolve(first, count):
        for g in range(GROUPS):
            for block in range(CONV // HEAD):
                total = jnp.zeros((count, HEAD), F32)
                for tap in range(4):
                    weight = conv_weight[tap, g : g + 1, block * HEAD : (block + 1) * HEAD].astype(F32)
                    total = total + weight * ext[4 * g + block, pl.ds(first + 5 + tap, count), :]
                value = silu(total)
                rows = pl.ds(first, count)
                if block < 2:
                    norm = lax.rsqrt(jnp.sum(value * value, -1, keepdims=True) + EPSILON)
                    if block == 0:
                        qn[g, rows, :] = (value * (norm * HEAD**-0.5)).astype(BF16)
                    else:
                        kn[g, rows, :] = (value * norm).astype(BF16)
                else:
                    vn[2 * g + block - 2, rows, :] = value.astype(BF16)

    convolve(HALO, ROWS - HALO)
    pl.when(seq > 0)(send_halo.wait_recv)

    @pl.when(seq == 0)
    def _():
        halo_in[...] = jnp.zeros_like(halo_in)

    for block in range(8):
        ext[block, 0:8, :] = halo_in[:, block * HEAD : (block + 1) * HEAD].astype(F32)[HALO - 8 :]
    convolve(0, HALO)

    row = lax.broadcasted_iota(jnp.int32, (HEAD, HEAD), 0)
    col = lax.broadcasted_iota(jnp.int32, (HEAD, HEAD), 1)
    on_lower = col <= row
    below_diag = col < row
    unit = jnp.where(col == row, 1.0, 0.0)
    unit_b = unit.astype(BF16)
    masks = []
    b = 1
    while b < HEAD:
        keep = (lax.div(row, 2 * b) == lax.div(col, 2 * b)) & (lax.div(row, b) != lax.div(col, b)) & below_diag
        masks.append(jnp.where(keep, 1.0, 0.0).astype(BF16))
        b *= 2

    parts = [pl.ds(0, HEAD), pl.ds(HEAD, HEAD)]
    inner = []
    for g in range(GROUPS):
        inner.append(matmul_t(jnp.concatenate([kn[g], qn[g]], 0), kn[g]))
    systems, scores = [], []
    for h in range(VALUE_HEADS):
        g, r = divmod(h, 2)
        lane_b, lane_c = 4 * g + r, 4 * g + 2 + r
        beta = gates[0][:, lane_b : lane_b + 1]
        cum = gates[1][:, lane_c : lane_c + 1]
        cum_t = cumulative_t[lane_c : lane_c + 1, :]
        system, score = {}, {}
        for i, j in ((0, 0), (1, 0), (1, 1)):
            ri, cj = slice(i * HEAD, (i + 1) * HEAD), slice(j * HEAD, (j + 1) * HEAD)
            gap = cum[ri] - cum_t[:, cj]
            if i == j:
                ratio = jnp.where(on_lower, jnp.exp(jnp.where(on_lower, gap, 0.0)), 0.0)
            else:
                ratio = jnp.exp(gap)
            system[i, j] = (beta[ri] * ratio * inner[g][ri, cj]).astype(BF16)
            score[i, j] = (ratio * inner[g][ROWS + i * HEAD : ROWS + (i + 1) * HEAD, cj]).astype(BF16)
        systems.append(system)
        scores.append(score)
    inverses = {(h, i): unit_b - masks[0] * systems[h][i, i] for h in range(VALUE_HEADS) for i in range(2)}
    for mask in masks[1:]:
        halves = {
            key: matmul(mask * systems[key[0]][key[1], key[1]], inverses[key]).astype(BF16) for key in inverses
        }
        inverses = {key: inverses[key] - matmul(inverses[key], halves[key]).astype(BF16) for key in inverses}

    solved = []
    for h in range(VALUE_HEADS):
        g, r = divmod(h, 2)
        lane_b, lane_c = 4 * g + r, 4 * g + 2 + r
        beta = gates[0][:, lane_b : lane_b + 1]
        cum = gates[1][:, lane_c : lane_c + 1]
        right = jnp.concatenate(
            [beta * jnp.exp(cum) * kn[g].astype(F32), beta * vn[h].astype(F32)], 1
        )
        first = matmul(inverses[h, 0], right[:HEAD].astype(BF16)).astype(BF16)
        second = right[HEAD:] - matmul(systems[h][1, 0], first)
        second = matmul(inverses[h, 1], second.astype(BF16)).astype(BF16)
        both = jnp.concatenate([first, second], 0)
        solved.append(both)
        last = cum[ROWS - 1 :, :]
        end_keys = (jnp.exp(last - cum) * kn[g].astype(F32)).astype(BF16)
        grown = lax.dot_general(end_keys, both, (((0,), (0,)), ((), ())), preferred_element_type=F32)
        change = (jnp.exp(last) - 1.0) * unit - grown[:, :HEAD]
        maps[h] = jnp.concatenate([change, grown[:, HEAD:]], 1).astype(BF16)
        row_copy = remote(
            maps.at[h], row_maps.at[x], row_send.at[h], row_recv.at[x], (z * NX + h, head)
        )
        pl.when(x != h)(row_copy.start)
        pending.append(functools.partial(pl.when(x != h), row_copy.wait_send))

        @pl.when(x == h)
        def _():
            row_maps[h] = maps[h]


    for h in range(VALUE_HEADS):
        g, r = divmod(h, 2)
        lane_c = 4 * g + 2 + r
        cum = gates[1][:, lane_c : lane_c + 1]
        top = matmul(scores[h][0, 0], solved[h][:HEAD])
        low = matmul(jnp.concatenate([scores[h][1, 0], scores[h][1, 1]], 1), solved[h])
        out = jnp.concatenate([top, low], 0)
        qeff[h] = (jnp.exp(cum) * qn[g].astype(F32) - out[:, :HEAD]).astype(BF16)
        loc[h] = out[:, HEAD:]

    for g in range(GROUPS):
        j = 3 * g + 2
        part = acc[j] + matmul(tokens_of(6, 2), w_in[6 * FEATURES :, j * 256 : (j + 1) * 256])
        gate = part.astype(BF16).astype(F32)
        out_gate[g] = silu(gate)

    for i in range(NX):
        row_copy = remote(maps.at[0], row_maps.at[i], row_send.at[0], row_recv.at[i], row_device(1))
        pl.when(x != i)(row_copy.wait_recv)

    prefix = [row_maps[0].astype(F32)]
    for i in range(1, NX):
        previous = prefix[-1]
        change = row_maps[i]
        prefix.append(previous + change.astype(F32) + matmul(change[:, :HEAD], previous.astype(BF16)))
    total = prefix[-1].astype(BF16)
    row_total[0] = total[:, :HEAD]
    row_total[1] = total[:, HEAD:]

    def apply(change, shift, before):
        return before + shift.astype(F32) + matmul(change, before.astype(BF16))

    def total_copy(d):
        return remote(
            row_total, totals_in.at[place], total_send.at[d - 1], total_recv.at[place], column_device(z + d)
        )

    def shift_copy(d):
        return remote(
            row_total.at[1], totals_in.at[0, 1], total_send.at[d - 1], total_recv.at[0], column_device(d)
        )

    def arrived(k):
        return remote(
            row_total, totals_in.at[k], total_send.at[0], total_recv.at[k], column_device(z)
        )

    def state_copy(d):
        return remote(
            state_out, state_in, state_send.at[d - 1], state_recv, column_device(z + d)
        )

    sends_total = {d: jnp.logical_and(place + d < QUAD, z > 0) for d in range(1, QUAD)}

    @pl.when(place < QUAD - 1)
    def _():
        pl.semaphore_wait(ready_sem, QUAD - 1 - place)

    for d in reversed(range(1, QUAD)):
        pl.when(z == 0)(shift_copy(d).start)
        pl.when(sends_total[d])(total_copy(d).start)
        pending.append(functools.partial(pl.when(z == 0), shift_copy(d).wait_send))
        pending.append(functools.partial(pl.when(sends_total[d]), total_copy(d).wait_send))

    def advance(k):
        arrived(k).wait_recv()
        state_before[...] = apply(totals_in[k, 0], totals_in[k, 1], state_before[...])

    @pl.when(z == 0)
    def _():
        state_before[...] = jnp.zeros_like(state_before)

    @pl.when(jnp.logical_and(z > 0, z < QUAD))
    def _():
        shift_copy(1).wait_recv()
        state_before[...] = totals_in[0, 1].astype(F32)
        for k in range(1, QUAD - 1):
            pl.when(place > k)(functools.partial(advance, k))

    @pl.when(base_row)
    def _():
        state_out[...] = apply(row_total[0], row_total[1], state_before[...]).astype(BF16)
        pl.semaphore_wait(ready_sem, QUAD)
        for d in range(1, QUAD + 1):
            state_copy(d).start()

    @pl.when(upper)
    def _():
        state_copy(1).wait_recv()
        state_before[...] = state_in[...].astype(F32)
        for k in range(QUAD - 1):
            pl.when(place > k)(functools.partial(advance, k))

    for d in range(1, QUAD + 1):
        pending.append(functools.partial(pl.when(base_row), state_copy(d).wait_send))
    state = state_before[...]
    row_states[0] = state.astype(BF16)
    for i in range(1, NX):
        before_i = prefix[i - 1]
        row_states[i] = apply(before_i[:, :HEAD].astype(BF16), before_i[:, HEAD:], state).astype(BF16)
    for r in range(1, NX):
        there = lax.rem(x + r, NX)
        copy = remote(row_states.at[there], states.at[x], back_send.at[r - 1], back_recv.at[r - 1], row_device(r))
        copy.start()
        pending.append(copy.wait_send)
    states[pl.ds(x, 1)] = row_states[pl.ds(x, 1)]
    for r in range(1, NX):
        here = lax.rem(x + NX - r, NX)
        remote(
            row_states.at[0], states.at[here], back_send.at[r - 1], back_recv.at[r - 1], row_device(r)
        ).wait_recv()

    gain = norm_gain[...]
    hidden = []
    for h in range(VALUE_HEADS):
        g, r = divmod(h, 2)
        attended = loc[h] + matmul(qeff[h], states[h])
        back = lax.rsqrt(jnp.mean(attended * attended, -1, keepdims=True) + EPSILON)
        gate = out_gate[g, :, r * HEAD : (r + 1) * HEAD]
        hidden.append((attended * back * gain * gate).astype(BF16))
    hidden = jnp.concatenate(hidden, 1)

    for r in (2, 1, 3, 0):
        slot = SLOT[(r, 1)]
        load_out[slot].wait()
        sib_out[r] = matmul(hidden, w_out[slot]).astype(BF16)
        remote(sib_out.at[r], sib_in.at[r], sib_send.at[r], sib_recv.at[r], sibling).start()
    for r in (2, 1, 3, 0):
        slot = SLOT[(r, 0)]
        load_out[slot].wait()
        own[r] = matmul(hidden, w_out[slot])

    def wait_sibling(r):
        remote(sib_out.at[r], sib_in.at[r], sib_send.at[r], sib_recv.at[r], sibling).wait_recv()

    ring = {
        r: remote(ring_out.at[r - 1], ring_in.at[r - 1], ring_send.at[r - 1], ring_recv.at[r - 1], device)
        for r, device in ((1, above), (2, across), (3, below))
    }
    for r in (2, 1, 3):
        wait_sibling(r)
        ring_out[r - 1] = (own[r] + sib_in[r].astype(F32)).astype(BF16)
        ring[r].start()
    wait_sibling(0)
    total = own[0] + sib_in[0].astype(F32)
    for r in (1, 3, 2):
        ring[r].wait_recv()
        total = total + ring_in[r - 1].astype(F32)
    out_ref[...] = total.astype(BF16)

    finish()
    for r in range(NY):
        remote(sib_out.at[r], sib_in.at[r], sib_send.at[r], sib_recv.at[r], sibling).wait_send()
    for copy in ring.values():
        copy.wait_send()


def per_device(
    tokens,
    in_weight,
    gate_weight,
    conv_weight,
    decay_scale,
    dt_bias,
    beta_shift,
    norm_gain,
    out_weight,
):
    anywhere = pl.BlockSpec(memory_space=pltpu.HBM)
    vmem = pl.BlockSpec(memory_space=pltpu.VMEM)
    dma = pltpu.SemaphoreType.DMA
    return pl.pallas_call(
        kernel,
        out_shape=jax.ShapeDtypeStruct((ROWS, FEATURES), BF16),
        in_specs=[anywhere] * 9,
        out_specs=vmem,
        scratch_shapes=[
            pltpu.VMEM((2 * VALUE_HEADS, 8 * FEATURES), BF16),
            pltpu.VMEM((4, GROUPS, CONV), BF16),
            pltpu.SMEM((VALUE_HEADS,), F32),
            pltpu.SMEM((VALUE_HEADS,), F32),
            pltpu.SMEM((VALUE_HEADS,), F32),
            pltpu.VMEM((1, HEAD), F32),
            pltpu.VMEM((8, ROWS, FEATURES), BF16),
            pltpu.VMEM((8 * FEATURES, GROUPS * GROUP), BF16),
            pltpu.VMEM((8, VALUE_HEADS * HEAD, FEATURES), BF16),
            pltpu.VMEM((TILES, ROWS, 256), F32),
            pltpu.VMEM((8, 8 + ROWS, HEAD), F32),
            pltpu.VMEM((HALO, GROUPS * CONV), BF16),
            pltpu.VMEM((HALO, GROUPS * CONV), BF16),
            pltpu.VMEM((2, ROWS, HEAD), F32),
            pltpu.VMEM((GROUPS, ROWS, HEAD), BF16),
            pltpu.VMEM((GROUPS, ROWS, HEAD), BF16),
            pltpu.VMEM((VALUE_HEADS, ROWS, HEAD), BF16),
            pltpu.VMEM((VALUE_HEADS, HEAD, 2 * HEAD), BF16),
            pltpu.VMEM((NX, HEAD, 2 * HEAD), BF16),
            pltpu.VMEM((2, HEAD, HEAD), BF16),
            pltpu.VMEM((QUAD - 1, 2, HEAD, HEAD), BF16),
            pltpu.VMEM((HEAD, HEAD), BF16),
            pltpu.VMEM((HEAD, HEAD), BF16),
            pltpu.VMEM((HEAD, HEAD), F32),
            pltpu.VMEM((GROUPS, ROWS, 2 * HEAD), F32),
            pltpu.VMEM((NX, HEAD, HEAD), BF16),
            pltpu.VMEM((VALUE_HEADS, HEAD, HEAD), BF16),
            pltpu.VMEM((VALUE_HEADS, ROWS, HEAD), F32),
            pltpu.VMEM((VALUE_HEADS, ROWS, HEAD), BF16),
            pltpu.VMEM((NY, ROWS, FEATURES), F32),
            pltpu.VMEM((NY, ROWS, FEATURES), BF16),
            pltpu.VMEM((NY, ROWS, FEATURES), BF16),
            pltpu.VMEM((NY - 1, ROWS, FEATURES), BF16),
            pltpu.VMEM((NY - 1, ROWS, FEATURES), BF16),
            dma,
            dma((6,)),
            dma((8,)),
            dma((8,)),
            dma((7,)),
            dma((8,)),
            dma((2,)),
            dma((NX,)),
            dma((NX,)),
            dma((QUAD - 1,)),
            dma((QUAD - 1,)),
            dma((QUAD,)),
            dma,
            pltpu.SemaphoreType.REGULAR,
            pltpu.SemaphoreType.REGULAR,
            dma((NX - 1,)),
            dma((NX - 1,)),
            dma((NY,)),
            dma((NY,)),
            dma((NY - 1,)),
            dma((NY - 1,)),
        ],
        compiler_params=pltpu.CompilerParams(
            collective_id=0, has_side_effects=True, vmem_limit_bytes=60 * 1024 * 1024
        ),
    )(
        tokens,
        in_weight,
        gate_weight.T,
        conv_weight,
        decay_scale,
        dt_bias,
        beta_shift,
        norm_gain.reshape(1, HEAD),
        out_weight,
    )


def solution(mesh):
    in_specs = (
        P("seq", "head"),
        P(None, "head"),
        P(None, "head"),
        P(None, "head", None),
        P("head"),
        P("head"),
        P("head"),
        P(),
        P("head", None),
    )
    out_specs = P("seq", "head")
    return jax.shard_map(
        per_device, mesh=mesh, in_specs=in_specs, out_specs=out_specs, check_vma=False
    )
```

time: 63.5 us -> 52.4 us (0.83)
  local copies, waits for them, and re-layouts: 7.49 us -> 1.57 us
  Pallas kernels: 55.3 us -> 50.4 us
    unnamed x16 -> x1, local copies, waits for them, and re-layouts: 7.49 us -> 1.57 us
    pallas_call x1, Pallas kernels: 55.3 us -> 50.4 us  [per_device(): pl.pallas_call(kernel, out_shape=jax.ShapeDtypeStruct((ROWS, FEATURES), B...]
where the time goes in v2:
time: 52.4 us; the launch traced here: 52 us
  Pallas kernels  50.4 us (96%)
  local copies, waits for them, and re-layouts  1.57 us (3%)
    pallas_call x1, Pallas kernels, per_device(): pl.pallas_call(kernel, out_shape=jax.ShapeDtypeStruct((ROWS, FEATURES), B...  50.4 us
    unnamed x1, local copies, waits for them, and re-layouts  1.57 us

profile of v2, /device:TPU:224, one launch (start us, length us, event | category | flops | bytes accessed | tf_op | source)
XLA Modules:
  0.0 52.0 jit_solution(13655679631781149224)
XLA Ops:
  0.0 50.4 %shard_map.91 = bf16[256,256]{1,0:T(8,128)(2,1)} custom-call(bf16[256,256]{1,0:T(8,128)(2,1)} %tokens_hbm.1, bf16[2048,1536]{1,0:T(8,128)(2,1)} %in_weight_hbm.1, bf16[8,2048]{1,0:T(8,128)(2,1)} %bitcast.2, bf16[4,2,512]{2,1,0:T(2,128)(2,1)} %conv_weight_hbm.1, f32[4]{0:T(128)} %decay_scale_hbm.1, f32[4]{0:T(128)} %dt_bias_hbm.1, f32[4]{0:T(128)} %beta_shift_hbm.1, ...), custom_call_target="tpu_custom_call" | custom-call | tf_op jit(solution)/shard_map/pallas_call | solution.py:595
  50.4 1.6 %copy.11 = bf16[256,256]{1,0:T(8,128)(2,1)} copy(bf16[256,256]{1,0:T(8,128)(2,1)} %shard_map.91) | data formatting | bytes 262144

commit v3 on v2

v3 whole, which is shorter than its diff:
```python
import functools

import jax
import jax.numpy as jnp
from jax import lax
from jax.experimental import pallas as pl
from jax.experimental.pallas import tpu as pltpu
from jax.sharding import PartitionSpec as P

F32 = jnp.float32
BF16 = jnp.bfloat16
EPSILON = 1e-06

ROWS = 256
HEAD = 128
FEATURES = 256
GROUPS = 2
VALUE_HEADS = 4
BLOCKS = ((0, 0), (1, 0), (1, 1))
TILES = 6
CONV = 512
GROUP = 768
HALO = 16
NX = 4
NZ = 8
NY = 4

CHIPS = (0, 1, 3, 2)


def matmul(a, b):
    return jnp.dot(a, b, preferred_element_type=F32)


def matmul_t(a, b):
    return lax.dot_general(a, b, (((1,), (1,)), ((), ())), preferred_element_type=F32)


def silu(v):
    return 0.5 * v * (1.0 + jnp.tanh(0.5 * v))


def kernel(
    tokens_hbm,
    in_weight_hbm,
    gate_weight_hbm,
    conv_weight_hbm,
    decay_scale_hbm,
    dt_bias_hbm,
    beta_shift_hbm,
    norm_gain_hbm,
    out_weight_hbm,
    out_ref,
    gate_weight,
    conv_weight,
    decay_scale,
    dt_bias,
    beta_shift,
    norm_gain,
    tok,
    w_in,
    w_out,
    acc,
    ext,
    halo_out,
    halo_in,
    gates,
    qn,
    kn,
    vn,
    maps,
    row_maps,
    prefix,
    row_total,
    total_in,
    pair_in,
    pair_out,
    state_in,
    state_out,
    state_before,
    out_gate,
    decays,
    row_states,
    states,
    loc,
    qeff,
    sib_out,
    sib_in,
    ring_out,
    ring_in,
    load_sem,
    small_sem,
    win_sem,
    wout_sem,
    tok_send,
    tok_recv,
    halo_sem,
    row_send,
    row_recv,
    total_send,
    total_recv,
    pair_send,
    pair_recv,
    state_send,
    state_recv,
    ready_sem,
    halo_ready_sem,
    back_send,
    back_recv,
    sib_send,
    sib_recv,
    ring_send,
    ring_recv,
):
    seq = lax.axis_index("seq")
    head = lax.axis_index("head")
    z, x = lax.div(seq, NX), lax.rem(seq, NX)
    y, c = lax.div(head, 2), lax.rem(head, 2)

    def chip_at(r):
        return lax.rem(y + r, NY)

    above = (seq, chip_at(1) * 2 + c)
    below = (seq, chip_at(3) * 2 + c)
    across = (seq, chip_at(2) * 2 + c)
    sibling = (seq, y * 2 + 1 - c)

    def remote(src, dst, send, recv, device):
        return pltpu.make_async_remote_copy(
            src_ref=src,
            dst_ref=dst,
            send_sem=send,
            recv_sem=recv,
            device_id=device,
            device_id_type=pl.DeviceIdType.MESH,
        )

    load_tok = pltpu.make_async_copy(tokens_hbm, tok.at[0, c], load_sem)
    load_tok.start()

    barrier = pltpu.get_barrier_semaphore()
    owner = c == 1

    def row_device(r, core):
        return (z * NX + lax.rem(x + r, NX), y * 2 + core)

    def column_device(there):
        return (there * NX + x, head)

    def signal(semaphore, device):
        pl.semaphore_signal(semaphore, inc=1, device_id=device, device_id_type=pl.DeviceIdType.MESH)

    odd = lax.rem(z, 2) == 1
    even = jnp.logical_not(odd)
    both_of = jnp.logical_and
    last_x = x == NX - 1
    not_top = z < NZ - 1
    next_row = ((z + 1) * NX, head)
    for device in [above, below, across, sibling] + [row_device(r, 1) for r in range(1, NX)]:
        signal(barrier, device)
    for r in range(1, NX):
        pl.when(owner)(functools.partial(signal, barrier, row_device(r, 0)))

    pl.when(both_of(owner, even))(functools.partial(signal, barrier, column_device(z + 1)))
    for d in (1, 2):
        pl.when(both_of(owner, both_of(odd, not_top)))(functools.partial(signal, barrier, column_device(z + d)))
    pl.when(both_of(owner, z == 4))(functools.partial(signal, barrier, column_device(z + 2)))
    for d in (3, 4):
        pl.when(both_of(owner, z == 3))(functools.partial(signal, barrier, column_device(z + d)))

    @pl.when(jnp.logical_and(last_x, not_top))
    def _():
        signal(barrier, next_row)

    def pair_of(r):
        return pl.ds(pl.multiple_of(chip_at(r) * 2 * FEATURES, 2 * FEATURES), 2 * FEATURES)

    load_in, load_out, load_small = [], [], []
    for i, r in enumerate(CHIPS):
        load_in.append(pltpu.make_async_copy(in_weight_hbm.at[pair_of(r)], w_in.at[i], win_sem.at[i]))
        load_out.append(
            pltpu.make_async_copy(out_weight_hbm.at[:, pair_of(r)], w_out.at[i], wout_sem.at[i])
        )
    for i, (source, target) in enumerate(
        (
            (gate_weight_hbm, gate_weight),
            (conv_weight_hbm, conv_weight),
            (decay_scale_hbm, decay_scale),
            (dt_bias_hbm, dt_bias),
            (beta_shift_hbm, beta_shift),
            (norm_gain_hbm, norm_gain),
        )
    ):
        load_small.append(pltpu.make_async_copy(source, target, small_sem.at[i]))
    for copy in load_in:
        copy.start()

    greeted = 7 + jnp.where(owner, 3 + lax.rem(z, 2) + jnp.where(z >= 2, 1, 0) + jnp.where(z >= 6, 1, 0) + jnp.where(z == 6, 1, 0), 0)
    greeted = greeted + jnp.where(jnp.logical_and(x == 0, z > 0), 1, 0)
    pl.semaphore_wait(barrier, greeted)

    pl.when(both_of(owner, odd))(functools.partial(signal, ready_sem, column_device(z - 1)))
    pl.when(both_of(owner, both_of(z >= 2, z < 4)))(functools.partial(signal, ready_sem, column_device(1)))
    pl.when(both_of(owner, z >= 4))(functools.partial(signal, ready_sem, column_device(3)))
    pl.when(both_of(owner, z >= 6))(functools.partial(signal, ready_sem, column_device(5)))
    pl.when(both_of(owner, z == 6))(functools.partial(signal, ready_sem, column_device(4)))

    @pl.when(jnp.logical_and(x == 0, z > 0))
    def _():
        signal(halo_ready_sem, ((z - 1) * NX + NX - 1, head))

    load_tok.wait()

    pending = []

    def finish():
        for wait in pending:
            wait()

    sends = []

    def send_tok(source, target, device):
        copy = remote(
            tok.at[source, c], tok.at[target, c], tok_send.at[len(sends)], tok_recv.at[target, c], device
        )
        copy.start()
        sends.append(copy)

    def wait_tok(i, core):
        remote(tok.at[i, core], tok.at[i, core], tok_send.at[0], tok_recv.at[i, core], sibling).wait_recv()

    up, down, far = CHIPS.index(1), CHIPS.index(3), CHIPS.index(2)
    send_tok(0, down, above)
    send_tok(0, up, below)
    send_tok(0, far, across)
    send_tok(0, 0, sibling)
    for copy in load_small + load_out:
        copy.start()

    def tokens_of(i):
        return jnp.concatenate([tok[i, 0], tok[i, 1]], 1)

    def project(chips, start):
        def tile(j, carry):
            columns = pl.ds(pl.multiple_of(j * 256, 256), 256)
            part = jnp.zeros((ROWS, 256), F32) if start else acc[j]
            for i in chips:
                part = part + matmul(tokens_of(i), w_in[i, :, columns])
            acc[j] = part
            return carry

        lax.fori_loop(0, TILES, tile, 0)

    wait_tok(0, 1 - c)
    load_in[0].wait()
    project((0,), True)
    for i in (down, up):
        wait_tok(i, c)
        send_tok(i, i, sibling)
    load_in[up].wait()
    load_in[down].wait()
    wait_tok(down, 1 - c)
    wait_tok(up, 1 - c)
    project((up, down), False)
    for copy in load_small:
        copy.wait()

    def gating_of(i):
        weight = gate_weight[:, pair_of(CHIPS[i])]
        weight = jnp.concatenate([weight, jnp.zeros((HEAD - weight.shape[0], 2 * FEATURES), BF16)], 0)
        return matmul_t(tokens_of(i), weight)

    gating = gating_of(0) + gating_of(up) + gating_of(down)
    wait_tok(far, c)
    send_tok(far, far, sibling)
    load_in[far].wait()
    wait_tok(far, 1 - c)
    pending.extend(copy.wait_send for copy in sends)

    def convolved(rows):
        for g in range(GROUPS):
            for i in range(2):
                j = 3 * g + i
                lhs = jnp.concatenate([tok[far, 0, rows], tok[far, 1, rows]], 1)
                part = acc[j, rows] + matmul(lhs, w_in[far, :, j * 256 : (j + 1) * 256])
                for block in range(2):
                    yield 4 * g + 2 * i + block, part[:, block * HEAD : (block + 1) * HEAD].astype(BF16)

    for block, columns in convolved(pl.ds(ROWS - HALO, HALO)):
        halo_out[:, block * HEAD : (block + 1) * HEAD] = columns
    next_seq = lax.rem(seq + 1, NX * NZ)
    send_halo = remote(halo_out, halo_in, halo_sem.at[0], halo_sem.at[1], (next_seq, head))

    @pl.when(jnp.logical_and(last_x, not_top))
    def _():
        pl.semaphore_wait(halo_ready_sem, 1)

    pl.when(seq < NX * NZ - 1)(send_halo.start)
    pending.append(lambda: pl.when(seq < NX * NZ - 1)(send_halo.wait_send))
    for block, columns in convolved(pl.ds(0, ROWS)):
        ext[block, 8:, :] = columns.astype(F32)

    gating = gating + gating_of(far)
    lane = lax.broadcasted_iota(jnp.int32, (1, HEAD), 1)
    shift = jnp.zeros((1, HEAD), F32)
    bias = jnp.zeros((1, HEAD), F32)
    scale = jnp.zeros((1, HEAD), F32)
    for h in range(VALUE_HEADS):
        g, r = divmod(h, 2)
        shift = jnp.where(lane == 4 * g + r, beta_shift[h], shift)
        bias = jnp.where(lane == 4 * g + 2 + r, dt_bias[h], bias)
        scale = jnp.where(lane == 4 * g + 2 + r, decay_scale[h], scale)
    strength = jax.nn.sigmoid(gating - shift)
    shifted = gating + bias
    softplus = jnp.maximum(shifted, 0.0) + jnp.log1p(jnp.exp(-jnp.abs(shifted)))
    log_gate = -scale * softplus
    row_id = lax.broadcasted_iota(jnp.int32, (ROWS, ROWS), 0)
    col_id = lax.broadcasted_iota(jnp.int32, (ROWS, ROWS), 1)
    ones = jnp.where(col_id <= row_id, 1.0, 0.0).astype(BF16)
    cumulative = jnp.zeros((ROWS, HEAD), F32)
    rest = log_gate
    for _ in range(3):
        piece = rest.astype(BF16)
        cumulative = cumulative + matmul(ones, piece)
        rest = rest - piece.astype(F32)
    cumulative_t = jnp.transpose(cumulative)
    gates[0] = strength
    gates[1] = cumulative

    def convolve(first, count):
        for g in range(GROUPS):
            for block in range(CONV // HEAD):
                total = jnp.zeros((count, HEAD), F32)
                for tap in range(4):
                    weight = conv_weight[tap, g : g + 1, block * HEAD : (block + 1) * HEAD].astype(F32)
                    total = total + weight * ext[4 * g + block, pl.ds(first + 5 + tap, count), :]
                value = silu(total)
                rows = pl.ds(first, count)
                if block < 2:
                    norm = lax.rsqrt(jnp.sum(value * value, -1, keepdims=True) + EPSILON)
                    if block == 0:
                        qn[g, rows, :] = (value * (norm * HEAD**-0.5)).astype(BF16)
                    else:
                        kn[g, rows, :] = (value * norm).astype(BF16)
                else:
                    vn[2 * g + block - 2, rows, :] = value.astype(BF16)

    convolve(HALO, ROWS - HALO)
    for g in range(GROUPS):
        j = 3 * g + 2
        part = acc[j] + matmul(tokens_of(far), w_in[far, :, j * 256 : (j + 1) * 256])
        out_gate[g] = silu(part.astype(BF16).astype(F32))
    row = lax.broadcasted_iota(jnp.int32, (HEAD, HEAD), 0)
    col = lax.broadcasted_iota(jnp.int32, (HEAD, HEAD), 1)
    on_lower = col <= row
    below_diag = col < row
    for h in range(VALUE_HEADS):
        g, r = divmod(h, 2)
        lane_c = 4 * g + 2 + r
        cum = cumulative[:, lane_c : lane_c + 1]
        cum_t = cumulative_t[lane_c : lane_c + 1, :]
        for n, (i, j) in enumerate(BLOCKS):
            gap = cum[i * HEAD : (i + 1) * HEAD] - cum_t[:, j * HEAD : (j + 1) * HEAD]
            if i == j:
                decays[h, n] = jnp.where(on_lower, jnp.exp(jnp.where(on_lower, gap, 0.0)), 0.0)
            else:
                decays[h, n] = jnp.exp(gap)

    pl.when(seq > 0)(send_halo.wait_recv)

    @pl.when(seq == 0)
    def _():
        halo_in[...] = jnp.zeros_like(halo_in)

    for block in range(8):
        ext[block, 0:8, :] = halo_in[:, block * HEAD : (block + 1) * HEAD].astype(F32)[HALO - 8 :]
    convolve(0, HALO)

    unit = jnp.where(col == row, 1.0, 0.0)
    unit_b = unit.astype(BF16)
    def within(wide, narrow):
        keep = (lax.div(row, wide) == lax.div(col, wide)) & (lax.div(row, narrow) != lax.div(col, narrow))
        return jnp.where(keep & below_diag, 1.0, 0.0).astype(BF16)

    masks = [within(4 * b, b) for b in (2, 8, 32)]

    parts = [pl.ds(0, HEAD), pl.ds(HEAD, HEAD)]
    inner = []
    for g in range(GROUPS):
        inner.append(matmul_t(jnp.concatenate([kn[g], qn[g]], 0), kn[g]))
    systems, scores = [], []
    for h in range(VALUE_HEADS):
        g, r = divmod(h, 2)
        lane_b, lane_c = 4 * g + r, 4 * g + 2 + r
        beta = gates[0][:, lane_b : lane_b + 1]
        system, score = {}, {}
        for n, (i, j) in enumerate(BLOCKS):
            ri, cj = slice(i * HEAD, (i + 1) * HEAD), slice(j * HEAD, (j + 1) * HEAD)
            ratio = decays[h, n]
            system[i, j] = (beta[ri] * ratio * inner[g][ri, cj]).astype(BF16)
            score[i, j] = (ratio * inner[g][ROWS + i * HEAD : ROWS + (i + 1) * HEAD, cj]).astype(BF16)
        systems.append(system)
        scores.append(score)
    keys = [(h, i) for h in range(VALUE_HEADS) for i in range(2)]
    pairs = within(2, 1)
    inverses = {key: unit_b - pairs * systems[key[0]][key[1], key[1]] for key in keys}
    for mask in masks:
        moved = {k: matmul(inverses[k], mask * systems[k[0]][k[1], k[1]]).astype(BF16) for k in keys}
        once = {k: inverses[k].astype(F32) - matmul(moved[k], inverses[k]) for k in keys}
        twice = {k: matmul(moved[k], moved[k]).astype(BF16) for k in keys}
        inverses = {k: (once[k] + matmul(twice[k], once[k].astype(BF16))).astype(BF16) for k in keys}

    solved = []
    for h in range(VALUE_HEADS):
        g, r = divmod(h, 2)
        lane_b, lane_c = 4 * g + r, 4 * g + 2 + r
        beta = gates[0][:, lane_b : lane_b + 1]
        cum = gates[1][:, lane_c : lane_c + 1]
        right = jnp.concatenate(
            [beta * jnp.exp(cum) * kn[g].astype(F32), beta * vn[h].astype(F32)], 1
        )
        first = matmul(inverses[h, 0], right[:HEAD].astype(BF16)).astype(BF16)
        across_parts = matmul(inverses[h, 1], systems[h][1, 0]).astype(BF16)
        second = matmul(inverses[h, 1], right[HEAD:].astype(BF16))
        second = (second - matmul(across_parts, first)).astype(BF16)
        both = jnp.concatenate([first, second], 0)
        solved.append(both)
        last = cum[ROWS - 1 :, :]
        end_keys = (jnp.exp(last - cum) * kn[g].astype(F32)).astype(BF16)
        grown = lax.dot_general(end_keys, both, (((0,), (0,)), ((), ())), preferred_element_type=F32)
        change = (jnp.exp(last) - 1.0) * unit - grown[:, :HEAD]
        maps[h] = jnp.concatenate([change, grown[:, HEAD:]], 1).astype(BF16)
        stays = jnp.logical_and(x == h, owner)
        row_copy = remote(
            maps.at[h], row_maps.at[c, x], row_send.at[h], row_recv.at[c, x], (z * NX + h, y * 2 + 1)
        )
        pl.when(jnp.logical_not(stays))(row_copy.start)
        pending.append(functools.partial(pl.when(jnp.logical_not(stays)), row_copy.wait_send))

        @pl.when(stays)
        def _():
            row_maps[1, h] = maps[h]

    for h in range(VALUE_HEADS):
        g, r = divmod(h, 2)
        lane_c = 4 * g + 2 + r
        cum = gates[1][:, lane_c : lane_c + 1]
        top = matmul(scores[h][0, 0], solved[h][:HEAD])
        low = matmul(jnp.concatenate([scores[h][1, 0], scores[h][1, 1]], 1), solved[h])
        out = jnp.concatenate([top, low], 0)
        qeff[h] = (jnp.exp(cum) * qn[g].astype(F32) - out[:, :HEAD]).astype(BF16)
        loc[h] = out[:, HEAD:]

    def compose(later, earlier):
        return earlier + later + matmul(later[:, :HEAD].astype(BF16), earlier.astype(BF16))

    def apply(change, shift, before):
        return before + shift.astype(F32) + matmul(change, before.astype(BF16))

    def total_copy(k):
        return remote(row_total.at[k], total_in.at[k], total_send.at[k], total_recv.at[k], column_device(z + 1))

    def shift_copy(k):
        return remote(
            row_total.at[k, 1], total_in.at[k, 1], total_send.at[k], total_recv.at[k], column_device(z + 1)
        )

    def skip_copy(k):
        return remote(row_total.at[k], pair_in.at[k], pair_send.at[k], pair_recv.at[k], column_device(z + 2))

    def pair_copy(k):
        return remote(pair_out.at[k], pair_in.at[k], pair_send.at[k], pair_recv.at[k], column_device(z + 2))

    def state_copy(d, k):
        return remote(
            state_out.at[k], state_in.at[k], state_send.at[k, d - 1], state_recv.at[k], column_device(z + d)
        )

    def back_copy(core, i):
        return remote(
            row_states.at[core, i], states.at[x], back_send.at[core, i], back_recv.at[x], (z * NX + i, y * 2 + core)
        )

    def leaves(core, i):
        return jnp.logical_not(jnp.logical_and(core == 1, x == i))

    @pl.when(owner)
    def _():
        answers = jnp.where(jnp.logical_or(odd, z == 4), 2, 1)

        @pl.when(z != 7)
        def _():
            pl.semaphore_wait(ready_sem, jnp.where(z == 3, 4, answers))


        for core in range(2):
            for i in range(NX):
                row_copy = remote(
                    maps.at[0], row_maps.at[core, i], row_send.at[0], row_recv.at[core, i], sibling
                )
                pl.when(leaves(core, i))(row_copy.wait_recv)
            row_map = [row_maps[core, i].astype(F32) for i in range(NX)]
            first_two = compose(row_map[1], row_map[0])
            last_two = compose(row_map[3], row_map[2])
            prefix[core, 0] = row_map[0]
            prefix[core, 1] = first_two
            prefix[core, 2] = compose(row_map[2], first_two)
            total = compose(last_two, first_two).astype(BF16)
            row_total[core, 0] = total[:, :HEAD]
            row_total[core, 1] = total[:, HEAD:]
            pl.when(z == 0)(shift_copy(core).start)
            pl.when(both_of(z > 0, jnp.logical_or(even, z == 5)))(total_copy(core).start)
            pl.when(z == 4)(skip_copy(core).start)

        def joined(ref, k):
            return jnp.concatenate([ref[k, 0], ref[k, 1]], 1).astype(F32)

        @pl.when(z == 0)
        def _():
            state_before[...] = jnp.zeros_like(state_before)

        @pl.when(z == 1)
        def _():
            for core in range(2):
                shift_copy(core).wait_recv()
                shift = total_in[core, 1].astype(F32)
                state_before[core] = shift
                state_out[core] = apply(row_total[core, 0], row_total[core, 1], shift).astype(BF16)
                state_copy(2, core).start()
                state_copy(1, core).start()

        @pl.when(both_of(even, both_of(z > 0, z < 6)))
        def _():
            for core in range(2):
                state_copy(1, core).wait_recv()
                state_before[core] = state_in[core].astype(F32)

        @pl.when(both_of(odd, both_of(z > 1, z < 6)))
        def _():
            for core in range(2):
                total_copy(core).wait_recv()
                pair = compose(joined(row_total, core), joined(total_in, core)).astype(BF16)
                pair_out[core, 0] = pair[:, :HEAD]
                pair_out[core, 1] = pair[:, HEAD:]
                pl.when(z == 5)(pair_copy(core).start)
            for core in range(2):
                state_copy(1, core).wait_recv()
                state = state_in[core].astype(F32)

                @pl.when(z == 3)
                def _():
                    state_out[core] = apply(pair_out[core, 0], pair_out[core, 1], state).astype(BF16)
                    for d in (3, 2, 4, 1):
                        state_copy(d, core).start()

                state_before[core] = apply(total_in[core, 0], total_in[core, 1], state)

        @pl.when(z == 6)
        def _():
            both = []
            for core in range(2):
                pair_copy(core).wait_recv()
                total_copy(core).wait_recv()
                both.append(compose(joined(total_in, core), joined(pair_in, core)))
            for core in range(2):
                state_copy(1, core).wait_recv()
                change = both[core][:, :HEAD].astype(BF16)
                state_before[core] = apply(change, both[core][:, HEAD:], state_in[core].astype(F32))

        @pl.when(z == 7)
        def _():
            for core in range(2):
                state_copy(1, core).wait_recv()
                pair_copy(core).wait_recv()
                total_copy(core).wait_recv()
                state = apply(pair_in[core, 0], pair_in[core, 1], state_in[core].astype(F32))
                state_before[core] = apply(total_in[core, 0], total_in[core, 1], state)

        for core in range(2):
            state = state_before[core]
            row_states[core, 0] = state.astype(BF16)
            for i in range(1, NX):
                before_i = prefix[core, i - 1]
                row_states[core, i] = apply(
                    before_i[:, :HEAD].astype(BF16), before_i[:, HEAD:], state
                ).astype(BF16)
            for i in range(NX):
                pl.when(leaves(core, i))(back_copy(core, i).start)
        states[pl.ds(x, 1)] = row_states[1, pl.ds(x, 1)]

    def wait_owner():
        for core in range(2):
            pl.when(z == 0)(shift_copy(core).wait_send)
            pl.when(both_of(z > 0, jnp.logical_or(even, z == 5)))(total_copy(core).wait_send)
            pl.when(z == 4)(skip_copy(core).wait_send)
            pl.when(z == 5)(pair_copy(core).wait_send)
            for d in (1, 2):
                pl.when(z == 1)(state_copy(d, core).wait_send)
            for d in range(1, 5):
                pl.when(z == 3)(state_copy(d, core).wait_send)
        for core in range(2):
            for i in range(NX):
                pl.when(leaves(core, i))(back_copy(core, i).wait_send)

    pending.append(lambda: pl.when(owner)(wait_owner))
    for h in range(VALUE_HEADS):
        arrival = remote(
            row_states.at[0, 0], states.at[h], back_send.at[0, 0], back_recv.at[h], sibling
        )
        pl.when(jnp.logical_not(jnp.logical_and(owner, x == h)))(arrival.wait_recv)

    gain = norm_gain[...]
    hidden = []
    for h in range(VALUE_HEADS):
        g, r = divmod(h, 2)
        attended = loc[h] + matmul(qeff[h], states[h])
        back = lax.rsqrt(jnp.mean(attended * attended, -1, keepdims=True) + EPSILON)
        gate = out_gate[g, :, r * HEAD : (r + 1) * HEAD]
        hidden.append((attended * back * gain * gate).astype(BF16))
    hidden = jnp.concatenate(hidden, 1)

    def partial_for(r, core):
        columns = pl.ds(pl.multiple_of(core * FEATURES, FEATURES), FEATURES)
        return matmul(hidden, w_out[CHIPS.index(r), :, columns])

    def sibling_copy(r):
        return remote(sib_out.at[r], sib_in.at[r], sib_send.at[r], sib_recv.at[r], sibling)

    ring = {
        r: remote(ring_out.at[r - 1], ring_in.at[r - 1], ring_send.at[r - 1], ring_recv.at[r - 1], device)
        for r, device in ((1, above), (2, across), (3, below))
    }
    for copy in load_out:
        copy.wait()
    def send_sibling(r):
        sib_out[r] = partial_for(r, 1 - c).astype(BF16)
        sibling_copy(r).start()

    def send_ring(r):
        mine = partial_for(r, c)
        sibling_copy(r).wait_recv()
        ring_out[r - 1] = (mine + sib_in[r].astype(F32)).astype(BF16)
        ring[r].start()

    send_sibling(2)
    send_sibling(1)
    send_ring(2)
    send_sibling(3)
    send_ring(1)
    send_ring(3)
    send_sibling(0)
    total = partial_for(0, c)
    sibling_copy(0).wait_recv()
    total = total + sib_in[0].astype(F32)
    for r in (1, 3, 2):
        ring[r].wait_recv()
        total = total + ring_in[r - 1].astype(F32)
    out_ref[...] = total.astype(BF16)

    finish()
    for r in range(NY):
        sibling_copy(r).wait_send()
    for copy in ring.values():
        copy.wait_send()


def per_device(
    tokens,
    in_weight,
    gate_weight,
    conv_weight,
    decay_scale,
    dt_bias,
    beta_shift,
    norm_gain,
    out_weight,
):
    anywhere = pl.BlockSpec(memory_space=pltpu.HBM)
    vmem = pl.BlockSpec(memory_space=pltpu.VMEM)
    dma = pltpu.SemaphoreType.DMA
    return pl.pallas_call(
        kernel,
        out_shape=pltpu.VMEM((ROWS, FEATURES), BF16),
        in_specs=[anywhere] * 9,
        out_specs=vmem,
        scratch_shapes=[
            pltpu.VMEM((2 * VALUE_HEADS, 8 * FEATURES), BF16),
            pltpu.VMEM((4, GROUPS, CONV), BF16),
            pltpu.SMEM((VALUE_HEADS,), F32),
            pltpu.SMEM((VALUE_HEADS,), F32),
            pltpu.SMEM((VALUE_HEADS,), F32),
            pltpu.VMEM((1, HEAD), F32),
            pltpu.VMEM((NY, 2, ROWS, FEATURES), BF16),
            pltpu.VMEM((NY, 2 * FEATURES, GROUPS * GROUP), BF16),
            pltpu.VMEM((NY, VALUE_HEADS * HEAD, 2 * FEATURES), BF16),
            pltpu.VMEM((TILES, ROWS, 256), F32),
            pltpu.VMEM((8, 8 + ROWS, HEAD), F32),
            pltpu.VMEM((HALO, GROUPS * CONV), BF16),
            pltpu.VMEM((HALO, GROUPS * CONV), BF16),
            pltpu.VMEM((2, ROWS, HEAD), F32),
            pltpu.VMEM((GROUPS, ROWS, HEAD), BF16),
            pltpu.VMEM((GROUPS, ROWS, HEAD), BF16),
            pltpu.VMEM((VALUE_HEADS, ROWS, HEAD), BF16),
            pltpu.VMEM((VALUE_HEADS, HEAD, 2 * HEAD), BF16),
            pltpu.VMEM((2, NX, HEAD, 2 * HEAD), BF16),
            pltpu.VMEM((2, NX - 1, HEAD, 2 * HEAD), F32),
            pltpu.VMEM((2, 2, HEAD, HEAD), BF16),
            pltpu.VMEM((2, 2, HEAD, HEAD), BF16),
            pltpu.VMEM((2, 2, HEAD, HEAD), BF16),
            pltpu.VMEM((2, 2, HEAD, HEAD), BF16),
            pltpu.VMEM((2, HEAD, HEAD), BF16),
            pltpu.VMEM((2, HEAD, HEAD), BF16),
            pltpu.VMEM((2, HEAD, HEAD), F32),
            pltpu.VMEM((GROUPS, ROWS, 2 * HEAD), F32),
            pltpu.VMEM((VALUE_HEADS, len(BLOCKS), HEAD, HEAD), F32),
            pltpu.VMEM((2, NX, HEAD, HEAD), BF16),
            pltpu.VMEM((VALUE_HEADS, HEAD, HEAD), BF16),
            pltpu.VMEM((VALUE_HEADS, ROWS, HEAD), F32),
            pltpu.VMEM((VALUE_HEADS, ROWS, HEAD), BF16),
            pltpu.VMEM((NY, ROWS, FEATURES), BF16),
            pltpu.VMEM((NY, ROWS, FEATURES), BF16),
            pltpu.VMEM((NY - 1, ROWS, FEATURES), BF16),
            pltpu.VMEM((NY - 1, ROWS, FEATURES), BF16),
            dma,
            dma((6,)),
            dma((NY,)),
            dma((NY,)),
            dma((7,)),
            dma((NY, 2)),
            dma((2,)),
            dma((NX,)),
            dma((2, NX)),
            dma((2,)),
            dma((2,)),
            dma((2,)),
            dma((2,)),
            dma((2, 4)),
            dma((2,)),
            pltpu.SemaphoreType.REGULAR,
            pltpu.SemaphoreType.REGULAR,
            dma((2, NX)),
            dma((NX,)),
            dma((NY,)),
            dma((NY,)),
            dma((NY - 1,)),
            dma((NY - 1,)),
        ],
        compiler_params=pltpu.CompilerParams(
            collective_id=0, has_side_effects=True, vmem_limit_bytes=60 * 1024 * 1024
        ),
    )(
        tokens,
        in_weight,
        gate_weight.T,
        conv_weight,
        decay_scale,
        dt_bias,
        beta_shift,
        norm_gain.reshape(1, HEAD),
        out_weight,
    )


def solution(mesh):
    in_specs = (
        P("seq", "head"),
        P(None, "head"),
        P(None, "head"),
        P(None, "head", None),
        P("head"),
        P("head"),
        P("head"),
        P(),
        P("head", None),
    )
    out_specs = P("seq", "head")
    return jax.shard_map(
        per_device, mesh=mesh, in_specs=in_specs, out_specs=out_specs, check_vma=False
    )
```

time: 52.4 us -> 50.2 us (0.958)
  local copies, waits for them, and re-layouts: 1.57 us -> 0.66 us
  Pallas kernels: 50.4 us -> 49.5 us
    pallas_call x1, Pallas kernels: 50.4 us -> 49.5 us  [per_device(): pl.pallas_call(kernel, out_shape=pltpu.VMEM((ROWS, FEATURES), BF16), in_s...]
    unnamed x1, local copies, waits for them, and re-layouts: 1.57 us -> 0.66 us
where the time goes in v3:
time: 50.2 us
  Pallas kernels  49.5 us (99%)
  local copies, waits for them, and re-layouts  0.66 us (1%)
    pallas_call x1, Pallas kernels, per_device(): pl.pallas_call(kernel, out_shape=pltpu.VMEM((ROWS, FEATURES), BF16), in_s...  49.5 us

profile of v3, /device:TPU:224, one launch (start us, length us, event | category | flops | bytes accessed | tf_op | source)
XLA Modules:
  0.0 50.2 jit_solution(1886979155863846834)
XLA Ops:
  0.0 49.5 %shard_map.91 = bf16[256,256]{1,0:T(8,128)(2,1)S(1)} custom-call(bf16[256,256]{1,0:T(8,128)(2,1)} %tokens_hbm.1, bf16[2048,1536]{1,0:T(8,128)(2,1)} %in_weight_hbm.1, bf16[8,2048]{1,0:T(8,128)(2,1)} %bitcast.2, bf16[4,2,512]{2,1,0:T(2,128)(2,1)} %conv_weight_hbm.1, f32[4]{0:T(128)} %decay_scale_hbm.1, f32[4]{0:T(128)} %dt_bias_hbm.1, f32[4]{0:T(128)} %beta_shift_hbm.1, ...), custom_call_target="tpu_custom_call" | custom-call | tf_op jit(solution)/shard_map/pallas_call | solution.py:681
  49.5 0.7 %copy.11 = bf16[256,256]{1,0:T(8,128)(2,1)} copy(bf16[256,256]{1,0:T(8,128)(2,1)S(1)} %shard_map.91) | data formatting | bytes 262144

commit v4 on v3

--- a/solution.py
+++ b/solution.py
@@ -94,6 +94,8 @@
     wout_sem,
     tok_send,
     tok_recv,
+    tail_send,
+    tail_recv,
     halo_sem,
     row_send,
     row_recv,
@@ -124,6 +126,7 @@
     below = (seq, chip_at(3) * 2 + c)
     across = (seq, chip_at(2) * 2 + c)
     sibling = (seq, y * 2 + 1 - c)
+    others = [(seq, chip_at(r) * 2 + 1 - c) for r in (1, 3, 2)]
 
     def remote(src, dst, send, recv, device):
         return pltpu.make_async_remote_copy(
@@ -156,7 +159,7 @@
     last_x = x == NX - 1
     not_top = z < NZ - 1
     next_row = ((z + 1) * NX, head)
-    for device in [above, below, across, sibling] + [row_device(r, 1) for r in range(1, NX)]:
+    for device in [above, below, across, sibling] + others + [row_device(r, 1) for r in range(1, NX)]:
         signal(barrier, device)
     for r in range(1, NX):
         pl.when(owner)(functools.partial(signal, barrier, row_device(r, 0)))
@@ -195,7 +198,7 @@
     for copy in load_in:
         copy.start()
 
-    greeted = 7 + jnp.where(owner, 3 + lax.rem(z, 2) + jnp.where(z >= 2, 1, 0) + jnp.where(z >= 6, 1, 0) + jnp.where(z == 6, 1, 0), 0)
+    greeted = 10 + jnp.where(owner, 3 + lax.rem(z, 2) + jnp.where(z >= 2, 1, 0) + jnp.where(z >= 6, 1, 0) + jnp.where(z == 6, 1, 0), 0)
     greeted = greeted + jnp.where(jnp.logical_and(x == 0, z > 0), 1, 0)
     pl.semaphore_wait(barrier, greeted)
 
@@ -219,17 +222,33 @@
 
     sends = []
 
+    body, tail = pl.ds(0, ROWS - HALO), pl.ds(ROWS - HALO, HALO)
+
     def send_tok(source, target, device):
         copy = remote(
-            tok.at[source, c], tok.at[target, c], tok_send.at[len(sends)], tok_recv.at[target, c], device
+            tok.at[source, c, body],
+            tok.at[target, c, body],
+            tok_send.at[len(sends)],
+            tok_recv.at[target, c],
+            device,
         )
         copy.start()
         sends.append(copy)
 
     def wait_tok(i, core):
-        remote(tok.at[i, core], tok.at[i, core], tok_send.at[0], tok_recv.at[i, core], sibling).wait_recv()
+        remote(
+            tok.at[i, core, body], tok.at[i, core, body], tok_send.at[0], tok_recv.at[i, core], sibling
+        ).wait_recv()
 
     up, down, far = CHIPS.index(1), CHIPS.index(3), CHIPS.index(2)
+    tail_targets = [(down, above), (down, others[0]), (up, below), (up, others[1])]
+    tail_targets += [(far, across), (far, others[2]), (0, sibling)]
+    for n, (target, device) in enumerate(tail_targets):
+        copy = remote(
+            tok.at[0, c, tail], tok.at[target, c, tail], tail_send.at[n], tail_recv.at[target, c], device
+        )
+        copy.start()
+        pending.append(copy.wait_send)
     send_tok(0, down, above)
     send_tok(0, up, below)
     send_tok(0, far, across)
@@ -251,14 +270,42 @@
 
         lax.fori_loop(0, TILES, tile, 0)
 
+    def wait_tail(i, core):
+        remote(
+            tok.at[i, core, tail], tok.at[i, core, tail], tail_send.at[0], tail_recv.at[i, core], sibling
+        ).wait_recv()
+
+    wait_tail(0, 1 - c)
     wait_tok(0, 1 - c)
     load_in[0].wait()
     project((0,), True)
+    for i in (up, down, far):
+        wait_tail(i, c)
+        wait_tail(i, 1 - c)
+    for i in (up, down, far):
+        load_in[i].wait()
+    for g in range(GROUPS):
+        for n in range(2):
+            columns = pl.ds((3 * g + n) * 256, 256)
+            part = jnp.zeros((HALO, 256), F32)
+            for i in range(NY):
+                rows = jnp.concatenate([tok[i, 0, tail], tok[i, 1, tail]], 1)
+                part = part + matmul(rows, w_in[i, :, columns])
+            halo_out[:, (2 * g + n) * 256 : (2 * g + n + 1) * 256] = part.astype(BF16)
+
     for i in (down, up):
         wait_tok(i, c)
         send_tok(i, i, sibling)
-    load_in[up].wait()
-    load_in[down].wait()
+
+    next_seq = lax.rem(seq + 1, NX * NZ)
+    send_halo = remote(halo_out, halo_in, halo_sem.at[0], halo_sem.at[1], (next_seq, head))
+
+    @pl.when(jnp.logical_and(last_x, not_top))
+    def _():
+        pl.semaphore_wait(halo_ready_sem, 1)
+
+    pl.when(seq < NX * NZ - 1)(send_halo.start)
+    pending.append(lambda: pl.when(seq < NX * NZ - 1)(send_halo.wait_send))
     wait_tok(down, 1 - c)
     wait_tok(up, 1 - c)
     project((up, down), False)
@@ -273,32 +320,16 @@
     gating = gating_of(0) + gating_of(up) + gating_of(down)
     wait_tok(far, c)
     send_tok(far, far, sibling)
-    load_in[far].wait()
     wait_tok(far, 1 - c)
     pending.extend(copy.wait_send for copy in sends)
 
-    def convolved(rows):
-        for g in range(GROUPS):
-            for i in range(2):
-                j = 3 * g + i
-                lhs = jnp.concatenate([tok[far, 0, rows], tok[far, 1, rows]], 1)
-                part = acc[j, rows] + matmul(lhs, w_in[far, :, j * 256 : (j + 1) * 256])
-                for block in range(2):
-                    yield 4 * g + 2 * i + block, part[:, block * HEAD : (block + 1) * HEAD].astype(BF16)
-
-    for block, columns in convolved(pl.ds(ROWS - HALO, HALO)):
-        halo_out[:, block * HEAD : (block + 1) * HEAD] = columns
-    next_seq = lax.rem(seq + 1, NX * NZ)
-    send_halo = remote(halo_out, halo_in, halo_sem.at[0], halo_sem.at[1], (next_seq, head))
-
-    @pl.when(jnp.logical_and(last_x, not_top))
-    def _():
-        pl.semaphore_wait(halo_ready_sem, 1)
-
-    pl.when(seq < NX * NZ - 1)(send_halo.start)
-    pending.append(lambda: pl.when(seq < NX * NZ - 1)(send_halo.wait_send))
-    for block, columns in convolved(pl.ds(0, ROWS)):
-        ext[block, 8:, :] = columns.astype(F32)
+    for g in range(GROUPS):
+        for n in range(2):
+            j = 3 * g + n
+            part = acc[j] + matmul(tokens_of(far), w_in[far, :, j * 256 : (j + 1) * 256])
+            for block in range(2):
+                columns = part[:, block * HEAD : (block + 1) * HEAD].astype(BF16)
+                ext[4 * g + 2 * n + block, 8:, :] = columns.astype(F32)
 
     gating = gating + gating_of(far)
     lane = lax.broadcasted_iota(jnp.int32, (1, HEAD), 1)
@@ -345,7 +376,15 @@
                 else:
                     vn[2 * g + block - 2, rows, :] = value.astype(BF16)
 
-    convolve(HALO, ROWS - HALO)
+    pl.when(seq > 0)(send_halo.wait_recv)
+
+    @pl.when(seq == 0)
+    def _():
+        halo_in[...] = jnp.zeros_like(halo_in)
+
+    for block in range(8):
+        ext[block, 0:8, :] = halo_in[:, block * HEAD : (block + 1) * HEAD].astype(F32)[HALO - 8 :]
+    convolve(0, ROWS)
     for g in range(GROUPS):
         j = 3 * g + 2
         part = acc[j] + matmul(tokens_of(far), w_in[far, :, j * 256 : (j + 1) * 256])
@@ -366,15 +405,6 @@
             else:
                 decays[h, n] = jnp.exp(gap)
 
-    pl.when(seq > 0)(send_halo.wait_recv)
-
-    @pl.when(seq == 0)
-    def _():
-        halo_in[...] = jnp.zeros_like(halo_in)
-
-    for block in range(8):
-        ext[block, 0:8, :] = halo_in[:, block * HEAD : (block + 1) * HEAD].astype(F32)[HALO - 8 :]
-    convolve(0, HALO)
 
     unit = jnp.where(col == row, 1.0, 0.0)
     unit_b = unit.astype(BF16)
@@ -499,18 +529,22 @@
                     maps.at[0], row_maps.at[core, i], row_send.at[0], row_recv.at[core, i], sibling
                 )
                 pl.when(leaves(core, i))(row_copy.wait_recv)
-            row_map = [row_maps[core, i].astype(F32) for i in range(NX)]
-            first_two = compose(row_map[1], row_map[0])
-            last_two = compose(row_map[3], row_map[2])
-            prefix[core, 0] = row_map[0]
-            prefix[core, 1] = first_two
-            prefix[core, 2] = compose(row_map[2], first_two)
-            total = compose(last_two, first_two).astype(BF16)
+        row_map = [[row_maps[core, i].astype(F32) for i in range(NX)] for core in range(2)]
+        first_two = [compose(row_map[core][1], row_map[core][0]) for core in range(2)]
+        last_two = [compose(row_map[core][3], row_map[core][2]) for core in range(2)]
+        for core in range(2):
+            total = compose(last_two[core], first_two[core]).astype(BF16)
             row_total[core, 0] = total[:, :HEAD]
             row_total[core, 1] = total[:, HEAD:]
+        for core in range(2):
             pl.when(z == 0)(shift_copy(core).start)
             pl.when(both_of(z > 0, jnp.logical_or(even, z == 5)))(total_copy(core).start)
+        for core in range(2):
             pl.when(z == 4)(skip_copy(core).start)
+        for core in range(2):
+            prefix[core, 0] = row_map[core][0]
+            prefix[core, 1] = first_two[core]
+            prefix[core, 2] = compose(row_map[core][2], first_two[core])
 
         def joined(ref, k):
             return jnp.concatenate([ref[k, 0], ref[k, 1]], 1).astype(F32)
@@ -550,7 +584,7 @@
                 @pl.when(z == 3)
                 def _():
                     state_out[core] = apply(pair_out[core, 0], pair_out[core, 1], state).astype(BF16)
-                    for d in (3, 2, 4, 1):
+                    for d in (4, 3, 2, 1):
                         state_copy(d, core).start()
 
                 state_before[core] = apply(total_in[core, 0], total_in[core, 1], state)
@@ -727,6 +761,8 @@
             dma((NY,)),
             dma((7,)),
             dma((NY, 2)),
+            dma((7,)),
+            dma((NY, 2)),
             dma((2,)),
             dma((NX,)),
             dma((2, NX)),

time: 50.2 us -> 49 us (0.976)
  Pallas kernels: 49.5 us -> 48 us
    pallas_call x1, Pallas kernels: 49.5 us -> 48 us  [per_device(): pl.pallas_call(kernel, out_shape=pltpu.VMEM((ROWS, FEATURES), BF16), in_s...]
where the time goes in v4:
time: 49 us; the launch traced here: 48.7 us
  Pallas kernels  48 us (98%)
  local copies, waits for them, and re-layouts  0.66 us (1%)
    pallas_call x1, Pallas kernels, per_device(): pl.pallas_call(kernel, out_shape=pltpu.VMEM((ROWS, FEATURES), BF16), in_s...  48 us

profile of v4, /device:TPU:224, one launch (start us, length us, event | category | flops | bytes accessed | tf_op | source)
XLA Modules:
  0.0 48.7 jit_solution(10484858075175873823)
XLA Ops:
  0.0 48.0 %shard_map.91 = bf16[256,256]{1,0:T(8,128)(2,1)S(1)} custom-call(bf16[256,256]{1,0:T(8,128)(2,1)} %tokens_hbm.1, bf16[2048,1536]{1,0:T(8,128)(2,1)} %in_weight_hbm.1, bf16[8,2048]{1,0:T(8,128)(2,1)} %bitcast.2, bf16[4,2,512]{2,1,0:T(2,128)(2,1)} %conv_weight_hbm.1, f32[4]{0:T(128)} %decay_scale_hbm.1, f32[4]{0:T(128)} %dt_bias_hbm.1, f32[4]{0:T(128)} %beta_shift_hbm.1, ...), custom_call_target="tpu_custom_call" | custom-call | tf_op jit(solution)/shard_map/pallas_call | solution.py:715
  48.0 0.7 %copy.11 = bf16[256,256]{1,0:T(8,128)(2,1)} copy(bf16[256,256]{1,0:T(8,128)(2,1)S(1)} %shard_map.91) | data formatting | bytes 262144

commit v5 on v4

--- a/solution.py
+++ b/solution.py
@@ -122,11 +122,10 @@
     def chip_at(r):
         return lax.rem(y + r, NY)
 
-    above = (seq, chip_at(1) * 2 + c)
-    below = (seq, chip_at(3) * 2 + c)
-    across = (seq, chip_at(2) * 2 + c)
+    above = (seq, chip_at(1) * 2 + 1 - c)
+    below = (seq, chip_at(3) * 2 + 1 - c)
+    across = (seq, chip_at(2) * 2 + 1 - c)
     sibling = (seq, y * 2 + 1 - c)
-    others = [(seq, chip_at(r) * 2 + 1 - c) for r in (1, 3, 2)]
 
     def remote(src, dst, send, recv, device):
         return pltpu.make_async_remote_copy(
@@ -158,8 +157,7 @@
     both_of = jnp.logical_and
     last_x = x == NX - 1
     not_top = z < NZ - 1
-    next_row = ((z + 1) * NX, head)
-    for device in [above, below, across, sibling] + others + [row_device(r, 1) for r in range(1, NX)]:
+    for device in [above, below, across, sibling] + [row_device(r, 1) for r in range(1, NX)]:
         signal(barrier, device)
     for r in range(1, NX):
         pl.when(owner)(functools.partial(signal, barrier, row_device(r, 0)))
@@ -171,9 +169,9 @@
     for d in (3, 4):
         pl.when(both_of(owner, z == 3))(functools.partial(signal, barrier, column_device(z + d)))
 
-    @pl.when(jnp.logical_and(last_x, not_top))
+    @pl.when(both_of(c == 0, both_of(last_x, not_top)))
     def _():
-        signal(barrier, next_row)
+        signal(barrier, ((z + 1) * NX + x, y * 2 + 1))
 
     def pair_of(r):
         return pl.ds(pl.multiple_of(chip_at(r) * 2 * FEATURES, 2 * FEATURES), 2 * FEATURES)
@@ -198,8 +196,8 @@
     for copy in load_in:
         copy.start()
 
-    greeted = 10 + jnp.where(owner, 3 + lax.rem(z, 2) + jnp.where(z >= 2, 1, 0) + jnp.where(z >= 6, 1, 0) + jnp.where(z == 6, 1, 0), 0)
-    greeted = greeted + jnp.where(jnp.logical_and(x == 0, z > 0), 1, 0)
+    greeted = 7 + jnp.where(owner, 3 + lax.rem(z, 2) + jnp.where(z >= 2, 1, 0) + jnp.where(z >= 6, 1, 0) + jnp.where(z == 6, 1, 0), 0)
+    greeted = greeted + jnp.where(both_of(owner, both_of(last_x, z > 0)), 1, 0)
     pl.semaphore_wait(barrier, greeted)
 
     pl.when(both_of(owner, odd))(functools.partial(signal, ready_sem, column_device(z - 1)))
@@ -208,9 +206,10 @@
     pl.when(both_of(owner, z >= 6))(functools.partial(signal, ready_sem, column_device(5)))
     pl.when(both_of(owner, z == 6))(functools.partial(signal, ready_sem, column_device(4)))
 
-    @pl.when(jnp.logical_and(x == 0, z > 0))
+    @pl.when(both_of(owner, both_of(last_x, z > 0)))
     def _():
-        signal(halo_ready_sem, ((z - 1) * NX + NX - 1, head))
+        for core in range(2):
+            signal(halo_ready_sem, ((z - 1) * NX + x, y * 2 + core))
 
     load_tok.wait()
 
@@ -224,16 +223,27 @@
 
     body, tail = pl.ds(0, ROWS - HALO), pl.ds(ROWS - HALO, HALO)
 
-    def send_tok(source, target, device):
+    def send_tok(source, target, core, device):
         copy = remote(
-            tok.at[source, c, body],
-            tok.at[target, c, body],
+            tok.at[source, core, body],
+            tok.at[target, core, body],
             tok_send.at[len(sends)],
-            tok_recv.at[target, c],
+            tok_recv.at[target, core],
             device,
         )
         copy.start()
         sends.append(copy)
+
+    def send_tail(n, source, target, core, device):
+        copy = remote(
+            tok.at[source, core, tail],
+            tok.at[target, core, tail],
+            tail_send.at[n],
+            tail_recv.at[target, core],
+            device,
+        )
+        copy.start()
+        pending.append(copy.wait_send)
 
     def wait_tok(i, core):
         remote(
@@ -241,18 +251,11 @@
         ).wait_recv()
 
     up, down, far = CHIPS.index(1), CHIPS.index(3), CHIPS.index(2)
-    tail_targets = [(down, above), (down, others[0]), (up, below), (up, others[1])]
-    tail_targets += [(far, across), (far, others[2]), (0, sibling)]
-    for n, (target, device) in enumerate(tail_targets):
-        copy = remote(
-            tok.at[0, c, tail], tok.at[target, c, tail], tail_send.at[n], tail_recv.at[target, c], device
-        )
-        copy.start()
-        pending.append(copy.wait_send)
-    send_tok(0, down, above)
-    send_tok(0, up, below)
-    send_tok(0, far, across)
-    send_tok(0, 0, sibling)
+    away = ((down, above), (up, below), (far, across), (0, sibling))
+    for n, (target, device) in enumerate(away):
+        send_tail(n, 0, target, c, device)
+    for target, device in away:
+        send_tok(0, target, c, device)
     for copy in load_small + load_out:
         copy.start()
 
@@ -279,9 +282,11 @@
     wait_tok(0, 1 - c)
     load_in[0].wait()
     project((0,), True)
+    for n, i in enumerate((up, down, far)):
+        wait_tail(i, 1 - c)
+        send_tail(4 + n, i, i, 1 - c, sibling)
     for i in (up, down, far):
         wait_tail(i, c)
-        wait_tail(i, 1 - c)
     for i in (up, down, far):
         load_in[i].wait()
     for g in range(GROUPS):
@@ -294,8 +299,8 @@
             halo_out[:, (2 * g + n) * 256 : (2 * g + n + 1) * 256] = part.astype(BF16)
 
     for i in (down, up):
-        wait_tok(i, c)
-        send_tok(i, i, sibling)
+        wait_tok(i, 1 - c)
+        send_tok(i, i, 1 - c, sibling)
 
     next_seq = lax.rem(seq + 1, NX * NZ)
     send_halo = remote(halo_out, halo_in, halo_sem.at[0], halo_sem.at[1], (next_seq, head))
@@ -306,8 +311,8 @@
 
     pl.when(seq < NX * NZ - 1)(send_halo.start)
     pending.append(lambda: pl.when(seq < NX * NZ - 1)(send_halo.wait_send))
-    wait_tok(down, 1 - c)
-    wait_tok(up, 1 - c)
+    wait_tok(down, c)
+    wait_tok(up, c)
     project((up, down), False)
     for copy in load_small:
         copy.wait()
@@ -318,9 +323,9 @@
         return matmul_t(tokens_of(i), weight)
 
     gating = gating_of(0) + gating_of(up) + gating_of(down)
+    wait_tok(far, 1 - c)
+    send_tok(far, far, 1 - c, sibling)
     wait_tok(far, c)
-    send_tok(far, far, sibling)
-    wait_tok(far, 1 - c)
     pending.extend(copy.wait_send for copy in sends)
 
     for g in range(GROUPS):
@@ -417,20 +422,18 @@
     parts = [pl.ds(0, HEAD), pl.ds(HEAD, HEAD)]
     inner = []
     for g in range(GROUPS):
-        inner.append(matmul_t(jnp.concatenate([kn[g], qn[g]], 0), kn[g]))
-    systems, scores = [], []
+        inner.append(matmul_t(kn[g], kn[g]))
+    systems = []
     for h in range(VALUE_HEADS):
         g, r = divmod(h, 2)
         lane_b, lane_c = 4 * g + r, 4 * g + 2 + r
         beta = gates[0][:, lane_b : lane_b + 1]
-        system, score = {}, {}
+        system = {}
         for n, (i, j) in enumerate(BLOCKS):
             ri, cj = slice(i * HEAD, (i + 1) * HEAD), slice(j * HEAD, (j + 1) * HEAD)
             ratio = decays[h, n]
             system[i, j] = (beta[ri] * ratio * inner[g][ri, cj]).astype(BF16)
-            score[i, j] = (ratio * inner[g][ROWS + i * HEAD : ROWS + (i + 1) * HEAD, cj]).astype(BF16)
         systems.append(system)
-        scores.append(score)
     keys = [(h, i) for h in range(VALUE_HEADS) for i in range(2)]
     pairs = within(2, 1)
     inverses = {key: unit_b - pairs * systems[key[0]][key[1], key[1]] for key in keys}
@@ -471,12 +474,17 @@
         def _():
             row_maps[1, h] = maps[h]
 
+    inner = [matmul_t(qn[g], kn[g]) for g in range(GROUPS)]
     for h in range(VALUE_HEADS):
         g, r = divmod(h, 2)
         lane_c = 4 * g + 2 + r
         cum = gates[1][:, lane_c : lane_c + 1]
-        top = matmul(scores[h][0, 0], solved[h][:HEAD])
-        low = matmul(jnp.concatenate([scores[h][1, 0], scores[h][1, 1]], 1), solved[h])
+        score = {}
+        for n, (i, j) in enumerate(BLOCKS):
+            ri, cj = slice(i * HEAD, (i + 1) * HEAD), slice(j * HEAD, (j + 1) * HEAD)
+            score[i, j] = (decays[h, n] * inner[g][ri, cj]).astype(BF16)
+        top = matmul(score[0, 0], solved[h][:HEAD])
+        low = matmul(jnp.concatenate([score[1, 0], score[1, 1]], 1), solved[h])
         out = jnp.concatenate([top, low], 0)
         qeff[h] = (jnp.exp(cum) * qn[g].astype(F32) - out[:, :HEAD]).astype(BF16)
         loc[h] = out[:, HEAD:]
@@ -613,12 +621,13 @@
         for core in range(2):
             state = state_before[core]
             row_states[core, 0] = state.astype(BF16)
+            pl.when(leaves(core, 0))(back_copy(core, 0).start)
             for i in range(1, NX):
                 before_i = prefix[core, i - 1]
                 row_states[core, i] = apply(
                     before_i[:, :HEAD].astype(BF16), before_i[:, HEAD:], state
                 ).astype(BF16)
-            for i in range(NX):
+            for i in range(1, NX):
                 pl.when(leaves(core, i))(back_copy(core, i).start)
         states[pl.ds(x, 1)] = row_states[1, pl.ds(x, 1)]
 
@@ -667,11 +676,11 @@
     for copy in load_out:
         copy.wait()
     def send_sibling(r):
-        sib_out[r] = partial_for(r, 1 - c).astype(BF16)
+        sib_out[r] = partial_for(r, 1 - c if r == 0 else c).astype(BF16)
         sibling_copy(r).start()
 
     def send_ring(r):
-        mine = partial_for(r, c)
+        mine = partial_for(r, 1 - c)
         sibling_copy(r).wait_recv()
         ring_out[r - 1] = (mine + sib_in[r].astype(F32)).astype(BF16)
         ring[r].start()
@@ -686,12 +695,12 @@
     total = partial_for(0, c)
     sibling_copy(0).wait_recv()
     total = total + sib_in[0].astype(F32)
-    for r in (1, 3, 2):
+    finish()
+    for r in (2, 1, 3):
         ring[r].wait_recv()
         total = total + ring_in[r - 1].astype(F32)
     out_ref[...] = total.astype(BF16)
 
-    finish()
     for r in range(NY):
         sibling_copy(r).wait_send()
     for copy in ring.values():

time: 49 us -> 48.3 us (0.986)
  Pallas kernels: 48 us -> 47.3 us
    pallas_call x1, Pallas kernels: 48 us -> 47.3 us  [per_device(): pl.pallas_call(kernel, out_shape=pltpu.VMEM((ROWS, FEATURES), BF16), in_s...]
where the time goes in v5:
time: 48.3 us; the launch traced here: 48 us
  Pallas kernels  47.3 us (98%)
  local copies, waits for them, and re-layouts  0.66 us (1%)
    pallas_call x1, Pallas kernels, per_device(): pl.pallas_call(kernel, out_shape=pltpu.VMEM((ROWS, FEATURES), BF16), in_s...  47.3 us

profile of v5, /device:TPU:224, one launch (start us, length us, event | category | flops | bytes accessed | tf_op | source)
XLA Modules:
  0.0 48.0 jit_solution(11333163137738781734)
XLA Ops:
  0.0 47.3 %shard_map.91 = bf16[256,256]{1,0:T(8,128)(2,1)S(1)} custom-call(bf16[256,256]{1,0:T(8,128)(2,1)} %tokens_hbm.1, bf16[2048,1536]{1,0:T(8,128)(2,1)} %in_weight_hbm.1, bf16[8,2048]{1,0:T(8,128)(2,1)} %bitcast.2, bf16[4,2,512]{2,1,0:T(2,128)(2,1)} %conv_weight_hbm.1, f32[4]{0:T(128)} %decay_scale_hbm.1, f32[4]{0:T(128)} %dt_bias_hbm.1, f32[4]{0:T(128)} %beta_shift_hbm.1, ...), custom_call_target="tpu_custom_call" | custom-call | tf_op jit(solution)/shard_map/pallas_call | solution.py:724
  47.3 0.7 %copy.11 = bf16[256,256]{1,0:T(8,128)(2,1)} copy(bf16[256,256]{1,0:T(8,128)(2,1)S(1)} %shard_map.91) | data formatting | bytes 262144

commit v6 on v5

--- a/solution.py
+++ b/solution.py
@@ -413,13 +413,13 @@
 
     unit = jnp.where(col == row, 1.0, 0.0)
     unit_b = unit.astype(BF16)
+
     def within(wide, narrow):
         keep = (lax.div(row, wide) == lax.div(col, wide)) & (lax.div(row, narrow) != lax.div(col, narrow))
         return jnp.where(keep & below_diag, 1.0, 0.0).astype(BF16)
 
     masks = [within(4 * b, b) for b in (2, 8, 32)]
 
-    parts = [pl.ds(0, HEAD), pl.ds(HEAD, HEAD)]
     inner = []
     for g in range(GROUPS):
         inner.append(matmul_t(kn[g], kn[g]))
@@ -443,26 +443,25 @@
         twice = {k: matmul(moved[k], moved[k]).astype(BF16) for k in keys}
         inverses = {k: (once[k] + matmul(twice[k], once[k].astype(BF16))).astype(BF16) for k in keys}
 
-    solved = []
-    for h in range(VALUE_HEADS):
+    def solve(h):
         g, r = divmod(h, 2)
         lane_b, lane_c = 4 * g + r, 4 * g + 2 + r
         beta = gates[0][:, lane_b : lane_b + 1]
         cum = gates[1][:, lane_c : lane_c + 1]
-        right = jnp.concatenate(
-            [beta * jnp.exp(cum) * kn[g].astype(F32), beta * vn[h].astype(F32)], 1
-        )
+        right = jnp.concatenate([beta * jnp.exp(cum) * kn[g].astype(F32), beta * vn[h].astype(F32)], 1)
         first = matmul(inverses[h, 0], right[:HEAD].astype(BF16)).astype(BF16)
         across_parts = matmul(inverses[h, 1], systems[h][1, 0]).astype(BF16)
         second = matmul(inverses[h, 1], right[HEAD:].astype(BF16))
         second = (second - matmul(across_parts, first)).astype(BF16)
         both = jnp.concatenate([first, second], 0)
-        solved.append(both)
         last = cum[ROWS - 1 :, :]
         end_keys = (jnp.exp(last - cum) * kn[g].astype(F32)).astype(BF16)
         grown = lax.dot_general(end_keys, both, (((0,), (0,)), ((), ())), preferred_element_type=F32)
         change = (jnp.exp(last) - 1.0) * unit - grown[:, :HEAD]
         maps[h] = jnp.concatenate([change, grown[:, HEAD:]], 1).astype(BF16)
+        return both
+
+    def hand_over(h):
         stays = jnp.logical_and(x == h, owner)
         row_copy = remote(
             maps.at[h], row_maps.at[c, x], row_send.at[h], row_recv.at[c, x], (z * NX + h, y * 2 + 1)
@@ -473,6 +472,12 @@
         @pl.when(stays)
         def _():
             row_maps[1, h] = maps[h]
+
+    solved = []
+    for heads in ((0, 1), (2, 3)):
+        solved += [solve(h) for h in heads]
+        for h in heads:
+            hand_over(h)
 
     inner = [matmul_t(qn[g], kn[g]) for g in range(GROUPS)]
     for h in range(VALUE_HEADS):

time: 48.3 us -> 47.4 us (0.981)
  Pallas kernels: 47.3 us -> 46.4 us
    pallas_call x1, Pallas kernels: 47.3 us -> 46.4 us  [per_device(): pl.pallas_call(kernel, out_shape=pltpu.VMEM((ROWS, FEATURES), BF16), in_s...]
where the time goes in v6:
time: 47.4 us; the launch traced here: 47 us
  Pallas kernels  46.4 us (98%)
  local copies, waits for them, and re-layouts  0.66 us (1%)
    pallas_call x1, Pallas kernels, per_device(): pl.pallas_call(kernel, out_shape=pltpu.VMEM((ROWS, FEATURES), BF16), in_s...  46.4 us

profile of v6, /device:TPU:224, one launch (start us, length us, event | category | flops | bytes accessed | tf_op | source)
XLA Modules:
  0.0 47.0 jit_solution(11562435013304879565)
XLA Ops:
  0.0 46.4 %shard_map.91 = bf16[256,256]{1,0:T(8,128)(2,1)S(1)} custom-call(bf16[256,256]{1,0:T(8,128)(2,1)} %tokens_hbm.1, bf16[2048,1536]{1,0:T(8,128)(2,1)} %in_weight_hbm.1, bf16[8,2048]{1,0:T(8,128)(2,1)} %bitcast.2, bf16[4,2,512]{2,1,0:T(2,128)(2,1)} %conv_weight_hbm.1, f32[4]{0:T(128)} %decay_scale_hbm.1, f32[4]{0:T(128)} %dt_bias_hbm.1, f32[4]{0:T(128)} %beta_shift_hbm.1, ...), custom_call_target="tpu_custom_call" | custom-call | tf_op jit(solution)/shard_map/pallas_call | solution.py:729
  46.4 0.7 %copy.11 = bf16[256,256]{1,0:T(8,128)(2,1)} copy(bf16[256,256]{1,0:T(8,128)(2,1)S(1)} %shard_map.91) | data formatting | bytes 262144

commit v7 on v6

--- a/solution.py
+++ b/solution.py
@@ -147,7 +147,7 @@
         return (z * NX + lax.rem(x + r, NX), y * 2 + core)
 
     def column_device(there):
-        return (there * NX + x, head)
+        return (lax.rem(there + NZ, NZ) * NX + x, head)
 
     def signal(semaphore, device):
         pl.semaphore_signal(semaphore, inc=1, device_id=device, device_id_type=pl.DeviceIdType.MESH)

time: 47.4 us -> 47.4 us (level)
  no operation moved by 1% of the time
where the time goes in v7:
time: 47.4 us; the launch traced here: 47 us
  Pallas kernels  46.4 us (98%)
  local copies, waits for them, and re-layouts  0.66 us (1%)
    pallas_call x1, Pallas kernels, per_device(): pl.pallas_call(kernel, out_shape=pltpu.VMEM((ROWS, FEATURES), BF16), in_s...  46.4 us

profile of v7, /device:TPU:224, one launch (start us, length us, event | category | flops | bytes accessed | tf_op | source)
XLA Modules:
  0.0 47.0 jit_solution(13244736109970925405)
XLA Ops:
  0.0 46.4 %shard_map.91 = bf16[256,256]{1,0:T(8,128)(2,1)S(1)} custom-call(bf16[256,256]{1,0:T(8,128)(2,1)} %tokens_hbm.1, bf16[2048,1536]{1,0:T(8,128)(2,1)} %in_weight_hbm.1, bf16[8,2048]{1,0:T(8,128)(2,1)} %bitcast.2, bf16[4,2,512]{2,1,0:T(2,128)(2,1)} %conv_weight_hbm.1, f32[4]{0:T(128)} %decay_scale_hbm.1, f32[4]{0:T(128)} %dt_bias_hbm.1, f32[4]{0:T(128)} %beta_shift_hbm.1, ...), custom_call_target="tpu_custom_call" | custom-call | tf_op jit(solution)/shard_map/pallas_call | solution.py:729
  46.4 0.7 %copy.11 = bf16[256,256]{1,0:T(8,128)(2,1)} copy(bf16[256,256]{1,0:T(8,128)(2,1)S(1)} %shard_map.91) | data formatting | bytes 262144

commit v8 on v7

--- a/solution.py
+++ b/solution.py
@@ -551,7 +551,7 @@
             row_total[core, 1] = total[:, HEAD:]
         for core in range(2):
             pl.when(z == 0)(shift_copy(core).start)
-            pl.when(both_of(z > 0, jnp.logical_or(even, z == 5)))(total_copy(core).start)
+            pl.when(both_of(z > 0, even))(total_copy(core).start)
         for core in range(2):
             pl.when(z == 4)(skip_copy(core).start)
         for core in range(2):
@@ -590,6 +590,8 @@
                 pair_out[core, 0] = pair[:, :HEAD]
                 pair_out[core, 1] = pair[:, HEAD:]
                 pl.when(z == 5)(pair_copy(core).start)
+            for core in range(2):
+                pl.when(z == 5)(total_copy(core).start)
             for core in range(2):
                 state_copy(1, core).wait_recv()
                 state = state_in[core].astype(F32)

time: 47.4 us -> 48.5 us (1.023)
  the two profiles are of different devices: /device:TPU:224 before, /device:TPU:193 now
where the time goes in v8:
time: 48.5 us
  Pallas kernels  47.8 us (99%)
  local copies, waits for them, and re-layouts  0.66 us (1%)
    pallas_call x1, Pallas kernels, per_device(): pl.pallas_call(kernel, out_shape=pltpu.VMEM((ROWS, FEATURES), BF16), in_s...  47.8 us

profile of v8, /device:TPU:193, one launch (start us, length us, event | category | flops | bytes accessed | tf_op | source)
XLA Modules:
  0.0 48.5 jit_solution(7241978281092638616)
XLA Ops:
  0.0 47.8 %shard_map.91 = bf16[256,256]{1,0:T(8,128)(2,1)S(1)} custom-call(bf16[256,256]{1,0:T(8,128)(2,1)} %tokens_hbm.1, bf16[2048,1536]{1,0:T(8,128)(2,1)} %in_weight_hbm.1, bf16[8,2048]{1,0:T(8,128)(2,1)} %bitcast.2, bf16[4,2,512]{2,1,0:T(2,128)(2,1)} %conv_weight_hbm.1, f32[4]{0:T(128)} %decay_scale_hbm.1, f32[4]{0:T(128)} %dt_bias_hbm.1, f32[4]{0:T(128)} %beta_shift_hbm.1, ...), custom_call_target="tpu_custom_call" | custom-call | tf_op jit(solution)/shard_map/pallas_call | solution.py:731
  47.8 0.7 %copy.11 = bf16[256,256]{1,0:T(8,128)(2,1)} copy(bf16[256,256]{1,0:T(8,128)(2,1)S(1)} %shard_map.91) | data formatting | bytes 262144
